TPU v7x, 512 devices: a whole 4x8x8 slice. The times are simulated.
512 devices in a mesh: row: 64 (over x, z, core), col: 8 (over y).
Axes of the slice: x: 4, y: 8, z: 8, core: 2. Of those that a mesh axis runs over, the one named last changes fastest.
Arguments:
- right_side: bfloat16 [31, 2048, 256], P(None, ('row', 'col')), may hold values from -6 to 6
- lower_blocks: bfloat16 [98, 2048, 2048], P(None, 'row', 'col'), may hold values from -0.0625 to 0.0625
- upper_blocks: bfloat16 [98, 2048, 2048], P(None, 'row', 'col'), may hold values from -0.0625 to 0.0625
- pivot_inverse: bfloat16 [31, 2048, 2048], P(None, 'row', 'col'), may hold values from -0.125 to 0.125
- widths: int32 [31], replicated, may hold values from 512 to 2048, as said below
- first_row: int32 [31, 4], replicated, may hold values from 0 to 1024, as said below
Outputs:
- solution: bfloat16 [31, 2048, 256], P(None, ('row', 'col'))
Inputs may be any that keep to these rules, and one draw needn't show every extreme that they name: Rows at or past widths[n] of supernode n are outside the supernode: right_side may hold any values there, and valid sets y and solution to zero in them. `first_row`: entry k of node n is used only for k below the depth of n.
All inputs are finite; a program needn't handle non-finite values.
Results may differ from a plain program's by a relative error of at most 0.008.
Values may be sent and summed in bfloat16 or wider, within the bound.
A program may use at most 64 MiB of HBM per device.

v0:
```python
import jax
import jax.numpy as jnp
from jax import lax
from jax.sharding import PartitionSpec as P

LEVELS = 5


def block_offsets():
    offsets = {}
    running = 0
    for tree_level in range(1, LEVELS):
        for hop_up in range(tree_level):
            offsets[tree_level, hop_up] = running
            running = running + 2**tree_level
    return offsets


def multiply(blocks, vectors):
    return jnp.einsum("nij,njr->nir", blocks, vectors, preferred_element_type=jnp.float32)


def solve_all(right_side, lower_blocks, upper_blocks, pivot_inverse, widths, first_row):
    offsets = block_offsets()
    row_rank = lax.axis_index("row")
    col_rank = lax.axis_index("col")
    proc_rows = lax.axis_size("row")
    proc_cols = lax.axis_size("col")
    piece_rows = right_side.shape[1]
    panel_rows = lower_blocks.shape[1]
    rhs_cols = right_side.shape[2]
    piece_index = jnp.arange(piece_rows, dtype=jnp.int32)
    own_rows = (row_rank * proc_cols + col_rank) * piece_rows + piece_index
    panel_index = row_rank * panel_rows + jnp.arange(panel_rows, dtype=jnp.int32)
    gathered_index = (
        (jnp.arange(proc_rows, dtype=jnp.int32)[:, None] * proc_cols + col_rank) * piece_rows
        + piece_index[None, :]
    ).reshape(-1)
    valid_own = (own_rows[None, :] < widths[:, None]).astype(jnp.float32)[:, :, None]
    couple_out = (panel_index[None, None, :] >= first_row[:, :, None]).astype(jnp.float32)
    couple_in = (gathered_index[None, None, :] >= first_row[:, :, None]).astype(jnp.bfloat16)
    pending = [
        jnp.zeros((2**tree_level, panel_rows, rhs_cols), jnp.float32)
        for tree_level in range(LEVELS)
    ]
    gathered_levels = [None] * LEVELS
    for tree_level in range(LEVELS - 1, -1, -1):
        first_node = 2**tree_level - 1
        span_nodes = 2**tree_level
        source = right_side[first_node : first_node + span_nodes].astype(jnp.float32)
        if tree_level < LEVELS - 1:
            source = source - lax.psum_scatter(
                pending[tree_level], "col", scatter_dimension=1, tiled=True
            )
        solved = (valid_own[first_node : first_node + span_nodes] * source).astype(jnp.bfloat16)
        spread = lax.all_gather(solved, "row", axis=1, tiled=True)
        gathered_levels[tree_level] = spread
        for hop_up in range(tree_level):
            block_start = offsets[tree_level, hop_up]
            product = multiply(lower_blocks[block_start : block_start + span_nodes], spread)
            product = product * couple_out[first_node : first_node + span_nodes, hop_up][:, :, None]
            target = tree_level - 1 - hop_up
            grouped = product.reshape(2**target, 2 ** (hop_up + 1), panel_rows, rhs_cols).sum(
                axis=1
            )
            pending[target] = pending[target] + grouped
    everything = jnp.concatenate(gathered_levels, axis=0)
    scaled = lax.psum_scatter(
        multiply(pivot_inverse, everything), "col", scatter_dimension=1, tiled=True
    )
    behind = [
        jnp.zeros((2**tree_level, panel_rows, rhs_cols), jnp.float32)
        for tree_level in range(LEVELS)
    ]
    answer = []
    for tree_level in range(LEVELS):
        first_node = 2**tree_level - 1
        span_nodes = 2**tree_level
        source = scaled[first_node : first_node + span_nodes]
        if tree_level > 0:
            source = source - lax.psum_scatter(
                behind[tree_level], "col", scatter_dimension=1, tiled=True
            )
        solved = (valid_own[first_node : first_node + span_nodes] * source).astype(jnp.bfloat16)
        answer.append(solved)
        if tree_level < LEVELS - 1:
            spread = lax.all_gather(solved, "row", axis=1, tiled=True)
            for lower_level in range(tree_level + 1, LEVELS):
                hop_up = lower_level - 1 - tree_level
                lower_first = 2**lower_level - 1
                lower_span = 2**lower_level
                repeated = jnp.repeat(spread, 2 ** (hop_up + 1), axis=0)
                masked = (
                    repeated * couple_in[lower_first : lower_first + lower_span, hop_up][:, :, None]
                )
                block_start = offsets[lower_level, hop_up]
                behind[lower_level] = behind[lower_level] + multiply(
                    upper_blocks[block_start : block_start + lower_span], masked
                )
    return jnp.concatenate(answer, axis=0)


def shards(right_side, lower_blocks, upper_blocks, pivot_inverse, widths, first_row):
    return solve_all(right_side, lower_blocks, upper_blocks, pivot_inverse, widths, first_row)


def solution(mesh):
    in_specs = (
        P(None, ("row", "col"), None),
        P(None, "row", "col"),
        P(None, "row", "col"),
        P(None, "row", "col"),
        P(),
        P(),
    )
    out_specs = P(None, ("row", "col"), None)
    return jax.shard_map(shards, mesh=mesh, in_specs=in_specs, out_specs=out_specs, check_vma=False)
```

profile of v0, /device:TPU:1, one launch (start us, length us, event | category | flops | bytes accessed | tf_op | source)
XLA Modules:
  0.0 1086.6 jit_solution(12423294207721480766)
XLA Ops:
  9.8 90.3 %all-gather.4.cloned.1.call-done = bf16[16,256,256]{2,0,1:T(8,128)(2,1)} async-done(((bf16[16,4,256]{2,0,1:T(8,128)(2,1)}), bf16[16,256,256]{2,0,1:T(8,128)(2,1)}) %all-gather.4.cloned.1.call-update) | async-done | bytes 2097168 | tf_op jit(solution)/shard_map/all_gather | solution.py:56
  100.0 2.5 bitcast_reduce_fusion.2
  103.6 30.5 %reduce-scatter.10.cloned.1.call-done = f32[8,4,256]{2,0,1:T(8,128)} async-done(((f32[8,32,256]{2,0,1:T(8,128)}), f32[8,4,256]{2,0,1:T(8,128)}) %reduce-scatter.10.cloned.1.call-update) | async-done | bytes 32784 | tf_op jit(solution)/shard_map/reduce_scatter | solution.py:52
  134.1 1.4 multiply_convert_fusion.1
  135.8 1.3 dynamic-slice
  137.9 1.7 bitcast_reduce_fusion.1
  139.6 1.7 bitcast_reduce_fusion
  141.3 1.7 fusion.14
  142.9 82.5 %all-gather.6.cloned.1.call-done = bf16[8,256,256]{2,0,1:T(8,128)(2,1)} async-done(((bf16[8,4,256]{2,0,1:T(8,128)(2,1)}), bf16[8,256,256]{2,0,1:T(8,128)(2,1)}) %all-gather.6.cloned.1.call-update) | async-done | bytes 1048592 | tf_op jit(solution)/shard_map/all_gather | solution.py:56
  225.4 1.6 bitcast_reduce_fusion.4
  227.8 1.6 bitcast_reduce_fusion.3
  229.4 1.6 fusion.16
  231.0 65.8 %all-reduce.12.cloned.1.call-done = f32[4,32,256]{2,1,0:T(8,128)} async-done(((f32[4,32,256]{2,1,0:T(8,128)}), f32[4,32,256]{2,1,0:T(8,128)}) %all-reduce.12.cloned.1.call-update) | async-done | bytes 131088
  297.7 57.0 %all_gather.31 = bf16[4,256,256]{2,0,1:T(4,128)(2,1)S(1)} all-gather(bf16[4,4,256]{2,0,1:T(4,128)(2,1)S(1)} %fusion.85), channel_id=1, replica_groups=mesh['row'=64,'col'=8] {'row'}, dimensions={1}, use_global_device_ids=true | all-gather | bytes 532480 | tf_op jit(solution)/shard_map/all_gather | solution.py:56
  357.5 65.4 %all-reduce.14.cloned.1.call-done = f32[2,32,256]{2,1,0:T(8,128)} async-done(((f32[2,32,256]{2,1,0:T(8,128)}), f32[2,32,256]{2,1,0:T(8,128)}) %all-reduce.14.cloned.1.call-update) | async-done | bytes 65552
  423.7 50.9 %all_gather.32 = bf16[2,256,256]{2,0,1:T(2,128)(2,1)S(1)} all-gather(bf16[2,4,256]{2,0,1:T(2,128)(2,1)S(1)} %fusion.89), channel_id=1, replica_groups=mesh['row'=64,'col'=8] {'row'}, dimensions={1}, use_global_device_ids=true | all-gather | bytes 266240 | tf_op jit(solution)/shard_map/all_gather | solution.py:56
  475.6 21.8 %all-reduce.2 = f32[1,32,256]{2,1,0:T(8,128)S(1)} all-reduce(f32[1,32,256]{2,1,0:T(8,128)S(1)} %add_bitcast_fusion), channel_id=5, replica_groups=mesh['row'=64,'col'=8] {'col'}, use_global_device_ids=true, to_apply=%region_13.0.clone | all-reduce | flops 8192 | bytes 65536
  497.5 50.4 %all_gather.33 = bf16[1,256,256]{2,0,1:T(2,128)(2,1)S(1)} all-gather(bf16[1,4,256]{2,0,1:T(2,128)(2,1)S(1)} %fusion.93), channel_id=1, replica_groups=mesh['row'=64,'col'=8] {'row'}, dimensions={1}, use_global_device_ids=true | all-gather | bytes 133120 | tf_op jit(solution)/shard_map/all_gather | solution.py:56
  549.0 1.8 convolution_bitcast_fusion
  552.3 70.6 %all-reduce.16.cloned.1.call-done = f32[31,32,256]{2,1,0:T(8,128)} async-done(((f32[31,32,256]{2,1,0:T(8,128)}), f32[31,32,256]{2,1,0:T(8,128)}) %all-reduce.16.cloned.1.call-update) | async-done | bytes 1015824
  623.7 50.2 %all_gather.34 = bf16[1,256,256]{2,0,1:T(2,128)(2,1)S(1)} all-gather(bf16[1,4,256]{2,0,1:T(2,128)(2,1)S(1)} %fusion.90), channel_id=1, replica_groups=mesh['row'=64,'col'=8] {'row'}, dimensions={1}, use_global_device_ids=true | all-gather | bytes 133120 | tf_op jit(solution)/shard_map/all_gather | solution.py:87
  677.2 64.6 %all-reduce.18.cloned.1.call-done = f32[2,32,256]{2,1,0:T(8,128)} async-done(((f32[2,32,256]{2,1,0:T(8,128)}), f32[2,32,256]{2,1,0:T(8,128)}) %all-reduce.18.cloned.1.call-update) | async-done | bytes 65552
  743.2 50.9 %all_gather.36 = bf16[2,256,256]{2,0,1:T(2,128)(2,1)S(1)} all-gather(bf16[2,4,256]{2,0,1:T(2,128)(2,1)S(1)} %fusion.87), channel_id=1, replica_groups=mesh['row'=64,'col'=8] {'row'}, dimensions={1}, use_global_device_ids=true | all-gather | bytes 266240 | tf_op jit(solution)/shard_map/all_gather | solution.py:87
  795.9 66.4 %all-reduce.20.cloned.1.call-done = f32[4,32,256]{2,1,0:T(8,128)} async-done(((f32[4,32,256]{2,1,0:T(8,128)}), f32[4,32,256]{2,1,0:T(8,128)}) %all-reduce.20.cloned.1.call-update) | async-done | bytes 131088
  863.2 57.0 %all_gather.37 = bf16[4,256,256]{2,0,1:T(4,128)(2,1)S(1)} all-gather(bf16[4,4,256]{2,0,1:T(4,128)(2,1)S(1)} %fusion.83), channel_id=1, replica_groups=mesh['row'=64,'col'=8] {'row'}, dimensions={1}, use_global_device_ids=true | all-gather | bytes 532480 | tf_op jit(solution)/shard_map/all_gather | solution.py:87
  920.3 1.1 bitcast_multiply_fusion.3
  923.4 27.8 %reduce-scatter.12.cloned.1.call-done = f32[8,4,256]{2,0,1:T(8,128)} async-done(((f32[8,32,256]{2,0,1:T(8,128)}), f32[8,4,256]{2,0,1:T(8,128)}) %reduce-scatter.12.cloned.1.call-update) | async-done | bytes 32784 | tf_op jit(solution)/shard_map/reduce_scatter | solution.py:81
  951.2 1.4 fusion.79
  955.9 85.8 %all-gather.8.cloned.1.call-done = bf16[8,256,256]{2,0,1:T(8,128)(2,1)} async-done(((bf16[8,4,256]{2,0,1:T(8,128)(2,1)}), bf16[8,256,256]{2,0,1:T(8,128)(2,1)}) %all-gather.8.cloned.1.call-update) | async-done | bytes 1048592 | tf_op jit(solution)/shard_map/all_gather | solution.py:87
  1041.7 1.4 copy.134
  1045.4 1.1 copy.135
  1047.4 30.7 %reduce-scatter.14.cloned.1.call-done = f32[16,4,256]{2,0,1:T(8,128)} async-done(((f32[16,32,256]{2,0,1:T(8,128)}), f32[16,4,256]{2,0,1:T(8,128)}) %reduce-scatter.14.cloned.1.call-update) | async-done | bytes 65552 | tf_op jit(solution)/shard_map/reduce_scatter | solution.py:81
  (155 shorter events, 31.7 us)
Async XLA Ops:
  6.5 542.4 %copy-start = (bf16[31,32,256]{2,1,0:T(8,128)(2,1)S(1)}, bf16[31,32,256]{2,1,0:T(8,128)(2,1)}, u32[]{:S(2)}) copy-start(bf16[31,32,256]{2,1,0:T(8,128)(2,1)} %param.9) | copy-start | bytes 1523716
  6.5 127.6 %slice-start = ((bf16[31,4,256]{2,1,0:T(4,128)(2,1)}), bf16[8,4,256]{2,1,0:T(4,128)(2,1)S(1)}, s32[]{:S(2)}) async-start(bf16[31,4,256]{2,1,0:T(4,128)(2,1)} %param.6), calls=%async_computation.14 | async-start | bytes 32768 | tf_op jit(solution)/shard_map/slice | solution.py:50
  6.5 93.5 %all-gather.4.cloned.1.call-start = ((), (), s32[]{:S(2)}) async-start(), calls=%async_computation.3 | async-start | bytes 2129920 | tf_op jit(solution)/shard_map/all_gather | solution.py:56
  7.4 130.4 %copy-start.19 = (f32[16,4]{0,1:T(4,128)}, f32[16,4]{0,1:T(4,128)S(1)}, u32[]{:S(2)}) copy-start(f32[16,4]{0,1:T(4,128)S(1)} %copy.94) | copy-start | bytes 772
  8.9 125.2 %reduce-scatter.10.cloned.1.call-start = ((), (), s32[]{:S(2)}) async-start(), calls=%async_computation.4 | async-start | bytes 294912 | tf_op jit(solution)/shard_map/reduce_scatter | solution.py:52
  100.0 37.9 %copy-start.1 = (bf16[16,256,256]{2,0,1:T(8,128)(2,1)S(1)}, bf16[16,256,256]{2,0,1:T(8,128)(2,1)}, u32[]{:S(2)}) copy-start(bf16[16,256,256]{2,0,1:T(8,128)(2,1)} %all-gather.4.cloned.1.call-done) | copy-start | bytes 6291460
  103.5 122.0 %all-gather.6.cloned.1.call-start = ((), (), s32[]{:S(2)}) async-start(), calls=%async_computation.5 | async-start | bytes 1064960 | tf_op jit(solution)/shard_map/all_gather | solution.py:56
  103.6 34.3 %copy-start.21 = (f32[8,4]{0,1:T(4,128)}, f32[8,4]{0,1:T(4,128)S(1)}, u32[]{:S(2)}) copy-start(f32[8,4]{0,1:T(4,128)S(1)} %copy.97) | copy-start | bytes 388
  135.6 161.3 %all-reduce.12.cloned.1.call-start = ((), (), s32[]{:S(2)}) async-start(), calls=%async_computation.9 | async-start | bytes 262144
  135.7 161.9 %copy-start.17 = (f32[4,4]{0,1:T(4,128)}, f32[4,4]{0,1:T(4,128)S(1)}, u32[]{:S(2)}) copy-start(f32[4,4]{0,1:T(4,128)S(1)} %copy.102) | copy-start | bytes 196
  135.8 287.8 %copy-start.15 = (f32[2,4]{0,1:T(4,128)}, f32[2,4]{0,1:T(4,128)S(1)}, u32[]{:S(2)}) copy-start(f32[2,4]{0,1:T(4,128)S(1)} %copy.108) | copy-start | bytes 100
  225.4 72.2 %slice-start.1 = ((bf16[31,4,256]{2,1,0:T(4,128)(2,1)}), bf16[4,4,256]{2,1,0:T(4,128)(2,1)S(1)}, s32[]{:S(2)}) async-start(bf16[31,4,256]{2,1,0:T(4,128)(2,1)} %param.6), calls=%async_computation.15 | async-start | bytes 16384 | tf_op jit(solution)/shard_map/slice | solution.py:50
  227.7 195.2 %all-reduce.14.cloned.1.call-start = ((), (), s32[]{:S(2)}) async-start(), calls=%async_computation.10 | async-start | bytes 131072
  229.4 194.3 %slice-start.2 = ((bf16[31,4,256]{2,1,0:T(4,128)(2,1)}), bf16[2,4,256]{2,1,0:T(4,128)(2,1)S(1)}, s32[]{:S(2)}) async-start(bf16[31,4,256]{2,1,0:T(4,128)(2,1)} %param.6), calls=%async_computation.16 | async-start | bytes 8192 | tf_op jit(solution)/shard_map/slice | solution.py:50
  229.4 268.0 %slice-start.3 = ((bf16[31,4,256]{2,1,0:T(4,128)(2,1)}), bf16[1,4,256]{2,1,0:T(4,128)(2,1)S(1)}, s32[]{:S(2)}) async-start(bf16[31,4,256]{2,1,0:T(4,128)(2,1)} %param.6), calls=%async_computation.17 | async-start | bytes 4096 | tf_op jit(solution)/shard_map/slice | solution.py:50
  356.4 266.6 %all-reduce.16.cloned.1.call-start = ((), (), s32[]{:S(2)}) async-start(), calls=%async_computation.11 | async-start | bytes 2031616
  497.4 50.6 %copy-start.3 = (bf16[8,256,256]{2,0,1:T(8,128)(2,1)S(1)}, bf16[8,256,256]{2,0,1:T(8,128)(2,1)}, u32[]{:S(2)}) copy-start(bf16[8,256,256]{2,0,1:T(8,128)(2,1)} %all-gather.6.cloned.1.call-done) | copy-start | bytes 3145732
  548.9 125.0 %copy-start.2 = (bf16[98,32,256]{2,1,0:T(8,128)(2,1)S(1)}, bf16[98,32,256]{2,1,0:T(8,128)(2,1)}, u32[]{:S(2)}) copy-start(bf16[98,32,256]{2,1,0:T(8,128)(2,1)} %param.8) | copy-start | bytes 4816900
  550.8 191.8 %copy-start.16 = (f32[2,4]{0,1:T(4,128)S(1)}, f32[2,4]{0,1:T(4,128)}, u32[]{:S(2)}) copy-start(f32[2,4]{0,1:T(4,128)} %copy-done.15) | copy-start | bytes 100
  550.8 191.1 %all-reduce.18.cloned.1.call-start = ((), (), s32[]{:S(2)}) async-start(), calls=%async_computation.12 | async-start | bytes 131072
  623.7 50.2 %copy-start.9 = (bf16[1,4,256]{2,0,1:T(2,128)(2,1)}, bf16[1,4,256]{2,0,1:T(2,128)(2,1)S(1)}, u32[]{:S(2)}) copy-start(bf16[1,4,256]{2,0,1:T(2,128)(2,1)S(1)} %fusion.90) | copy-start | bytes 6148
  674.9 187.5 %all-reduce.20.cloned.1.call-start = ((), (), s32[]{:S(2)}) async-start(), calls=%async_computation.13 | async-start | bytes 262144
  794.4 68.7 %copy-start.18 = (f32[4,4]{0,1:T(4,128)S(1)}, f32[4,4]{0,1:T(4,128)}, u32[]{:S(2)}) copy-start(f32[4,4]{0,1:T(4,128)} %copy-done.17) | copy-start | bytes 196
  795.3 156.0 %reduce-scatter.12.cloned.1.call-start = ((), (), s32[]{:S(2)}) async-start(), calls=%async_computation.6 | async-start | bytes 294912 | tf_op jit(solution)/shard_map/reduce_scatter | solution.py:81
  863.2 57.1 %copy-start.7 = (bf16[4,4,256]{2,0,1:T(4,128)(2,1)}, bf16[4,4,256]{2,0,1:T(4,128)(2,1)S(1)}, u32[]{:S(2)}) copy-start(bf16[4,4,256]{2,0,1:T(4,128)(2,1)S(1)} %fusion.83) | copy-start | bytes 24580
  922.5 119.2 %all-gather.8.cloned.1.call-start = ((), (), s32[]{:S(2)}) async-start(), calls=%async_computation.7 | async-start | bytes 1064960 | tf_op jit(solution)/shard_map/all_gather | solution.py:87
  952.7 125.4 %reduce-scatter.14.cloned.1.call-start = ((), (), s32[]{:S(2)}) async-start(), calls=%async_computation.8 | async-start | bytes 589824 | tf_op jit(solution)/shard_map/reduce_scatter | solution.py:81
  955.4 87.7 %copy-start.14 = (bf16[16,256]{1,0:T(8,128)(2,1)S(1)}, bf16[16,256]{1,0:T(8,128)(2,1)}, u32[]{:S(2)}) copy-start(bf16[16,256]{1,0:T(8,128)(2,1)} %get-tuple-element.6) | copy-start | bytes 24580
  1044.6 34.4 %copy-start.6 = (bf16[8,4,256]{2,0,1:T(8,128)(2,1)S(1)}, bf16[8,4,256]{2,0,1:T(8,128)(2,1)}, u32[]{:S(2)}) copy-start(bf16[8,4,256]{2,0,1:T(8,128)(2,1)} %fusion.79) | copy-start | bytes 49156
  1044.6 34.5 %copy-start.8 = (bf16[4,4,256]{2,0,1:T(4,128)(2,1)S(1)}, bf16[4,4,256]{2,0,1:T(4,128)(2,1)}, u32[]{:S(2)}) copy-start(bf16[4,4,256]{2,0,1:T(4,128)(2,1)} %copy-done.7) | copy-start | bytes 24580
  1044.6 34.5 %copy-start.10 = (bf16[1,4,256]{2,0,1:T(2,128)(2,1)S(1)}, bf16[1,4,256]{2,0,1:T(2,128)(2,1)}, u32[]{:S(2)}) copy-start(bf16[1,4,256]{2,0,1:T(2,128)(2,1)} %copy-done.9) | copy-start | bytes 6148
  1044.6 34.5 %copy-start.12 = (bf16[2,4,256]{2,0,1:T(2,128)(2,1)S(1)}, bf16[2,4,256]{2,0,1:T(2,128)(2,1)}, u32[]{:S(2)}) copy-start(bf16[2,4,256]{2,0,1:T(2,128)(2,1)} %copy-done.11) | copy-start | bytes 12292
  (7 other events, 101.2 us)
Sparse Core Ops, SparseCore 0:
  10.7 89.2 all-gather.3
  103.6 30.4 reduce-scatter.9
  138.0 87.4 all-gather.5
  227.9 68.9 all-reduce.11
  356.5 66.3 all-reduce.13
  550.9 71.9 all-reduce.15
  675.0 66.8 all-reduce.17
  795.4 66.8 all-reduce.19
  922.6 28.5 reduce-scatter.11
  954.4 87.2 all-gather.7
  1046.6 31.4 reduce-scatter.13
where the time goes:
time: 1090 us
  waiting for transfers between devices  681 us (62%)
  blocking collectives  338 us (31%)
  matrix products  22.5 us (2%)
  local copies, waits for them, and re-layouts  18.7 us (2%)
  between operations  14.5 us (1%)
  other arithmetic  11.7 us (1%)
    unnamed x16, waiting for transfers between devices  333 us
    all_gather x6, blocking collectives, solve_all(): spread = lax.all_gather(solved, 'row', axis=1, tiled=True)  316 us
    all_gather x3, waiting for transfers between devices, solve_all(): spread = lax.all_gather(solved, 'row', axis=1, tiled=True)  259 us
    reduce_scatter x2, waiting for transfers between devices, solve_all(): lax.psum_scatter(behind[tree_level], 'col', scatter_dimension=1, tiled=True)  58.5 us
    reduce_scatter x1, waiting for transfers between devices, solve_all(): lax.psum_scatter(pending[tree_level], 'col', scatter_dimension=1, tiled=T...  30.5 us
    dot_general x21, matrix products, multiply(): jnp.einsum('nij,njr->nir', blocks, vectors, preferred_element_type=jnp.fl...  22.5 us
    unnamed x1, blocking collectives  21.8 us
  transfers between devices with their start and end apart: 11, of which 11 were waited for; matrix products, arithmetic and copies ran while one was open for 2% of the time, Pallas kernels for 0%

commit v1 on v0

v1 whole, which is shorter than its diff:
```python
import functools

import jax
import jax.numpy as jnp
from jax import lax
from jax.experimental import pallas as pl
from jax.experimental.pallas import tpu as pltpu
from jax.sharding import PartitionSpec as P

MESH = pl.DeviceIdType.MESH
BF = jnp.bfloat16
F32 = jnp.float32
LEVELS = 5
NX, NZ, NC = 4, 8, 8
NQ = NX * NZ
GROUPS = [1, 1, 1, 2, 4]
GBASE = [8, 7, 6, 4, 0]
NGROUP = 9
GROUP = 16


def block_offsets():
    offsets = {}
    running = 0
    for tree_level in range(1, LEVELS):
        for hop_up in range(tree_level):
            offsets[tree_level, hop_up] = running
            running = running + 2**tree_level
    return offsets


OFF = block_offsets()


def forward_rows(t):
    rows, at = [], 0
    for hop in range(t):
        count = 32 * (2 if hop == 0 and t >= 2 else 1)
        rows.append((t - 1 - hop, at, count))
        at += count
    count = 32 * min(4, 2**t)
    rows.append((-1, at, count))
    return rows, at + count


def backward_rows(t):
    rows, at = [], 0
    for s in range(t + 1, LEVELS):
        count = 32 * min(4, 2**t) * 2 ** (s - t)
        rows.append((s, at, count))
        at += count
    return rows, at


FROWS = [forward_rows(t) for t in range(LEVELS)]
BROWS = [backward_rows(t) for t in range(LEVELS - 1)]


def kernel(rs_ref, widths_ref, first_ref, l_hbm, u_hbm, d_hbm, out_ref, scratch):
    row = lax.axis_index("row")
    col = lax.axis_index("col")
    x, z, core = row // 16, (row // 2) % 8, row % 2
    q = x * NZ + z
    other = 1 - core
    lw, uw, dw, sel, perm = (scratch[n] for n in ("lw", "uw", "dw", "sel", "perm"))
    fw, bw, pend, acc = (scratch[n] for n in ("fw", "bw", "pend", "acc"))
    gather, relay_sem, load_sem = scratch["gather"], scratch["relay_sem"], scratch["load_sem"]
    slabs, sums, ring_sem = scratch["slabs"], scratch["sums"], scratch["ring_sem"]

    loads = [
        pltpu.make_async_copy(src, dst, load_sem.at[i])
        for i, (src, dst) in enumerate(((l_hbm, lw), (u_hbm, uw), (d_hbm, dw)))
    ]
    for load in loads:
        load.start()

    barrier = pltpu.get_barrier_semaphore()

    def plane_peer(k):
        px, pz = (x + k // NZ) % NX, (z + k % NZ) % NZ
        return (px * NZ + pz) * 2 + core

    def signal(target):
        pl.semaphore_signal(barrier, inc=1, device_id=target, device_id_type=MESH)

    @pl.loop(1, NQ)
    def _(k):
        signal({"row": plane_peer(k)})

    @pl.loop(1, NC)
    def _(k):
        signal({"col": (col + k) % NC})

    signal({"row": q * 2 + other})

    row16 = lax.broadcasted_iota(jnp.int32, (GROUP, 256), 0)
    own_row = row * 32 + col * 4 + row16 % 4

    def valid(t, g):
        limit = jnp.zeros((GROUP, 256), jnp.int32)
        for j in range(min(4, 2**t)):
            limit = jnp.where(row16 // 4 == j, widths_ref[2**t - 1 + 4 * g + j], limit)
        return (own_row < limit).astype(F32)

    def piece(t, g):
        at = (GBASE[t] + g) * GROUP
        return slice(at, at + GROUP)

    for g in range(4):
        y = valid(4, g) * rs_ref[piece(4, g)].astype(F32)
        gather["f4"][g, core, q] = y.astype(BF)

    @pl.loop(0, 2)
    def _(h):
        @pl.loop(0, 8)
        def _(b):
            r = lax.broadcasted_iota(jnp.int32, (128, 512), 0) + b * 128
            s = lax.broadcasted_iota(jnp.int32, (128, 512), 1)
            p = (r % 256) // 4
            target = (p // 2) * 16 + (r // 256) * 4 + r % 4
            hit = jnp.logical_and(s == target, p % 2 == h)
            sel[h, pl.ds(pl.multiple_of(b * 128, 128), 128)] = hit.astype(F32).astype(BF)

    r = lax.broadcasted_iota(jnp.int32, (128, 128), 0)
    s = lax.broadcasted_iota(jnp.int32, (128, 128), 1)
    perm[...] = (s == ((r // 4) % 4) * 32 + (r // 16) * 4 + r % 4).astype(F32).astype(BF)
    for t in range(LEVELS - 1):
        pend[t][...] = jnp.zeros_like(pend[t])

    out_row = row * 32 + lax.broadcasted_iota(jnp.int32, (32, 256), 0)
    lane = lax.broadcasted_iota(jnp.int32, (32, 256), 1)
    in_row = (lane // 4) * 32 + col * 4 + lane % 4

    def mask(ref, index, t, hop):
        @pl.loop(0, 2**t)
        def _(n):
            keep = (index >= first_ref[2**t - 1 + n, hop]).astype(F32).astype(BF)
            ref[OFF[t, hop] + n] = ref[OFF[t, hop] + n] * keep

    def stack(ref, base, groups, members):
        return jnp.concatenate(
            [
                jnp.concatenate([ref[base + 4 * g + j] for j in members], axis=1)
                for g in range(groups)
            ],
            axis=0,
        )

    def expand_forward(t):
        groups = GROUPS[t]
        for target, at, count in FROWS[t][0]:
            if target >= 0:
                hop = t - 1 - target
                halves = count // 32
                per = min(4, 2**t) // halves
                jobs = [
                    (lw, OFF[t, hop], at + 32 * v, [v * per + w for w in range(per)])
                    for v in range(halves)
                ]
            else:
                jobs = [(dw, 2**t - 1, at + 32 * j, [j]) for j in range(count // 32)]
            for ref, base, first, members in jobs:
                left = stack(ref, base, groups, members)

                @pl.loop(0, 2)
                def _(h):
                    table = sel[h, members[0] * 256 : (members[-1] + 1) * 256]
                    wide = jnp.dot(left, table, preferred_element_type=F32).astype(BF)
                    for g in range(groups):
                        fw[t][g, h, first : first + 32] = wide[g * 32 : (g + 1) * 32]

    def expand_backward(t):
        for g in range(GROUPS[t]):
            for s, at, count in BROWS[t][0]:
                each = 2 ** (s - t)
                for j in range(min(4, 2**t)):
                    base = OFF[s, s - 1 - t] + (4 * g + j) * each
                    left = uw[base : base + each].reshape(each * 32, 256)
                    first = at + j * each * 32

                    @pl.loop(0, 2)
                    def _(h):
                        table = sel[h, j * 256 : (j + 1) * 256]
                        wide = jnp.dot(left, table, preferred_element_type=F32).astype(BF)
                        bw[t][g, h, first : first + each * 32] = wide

    def remote(src, dst, number, target):
        return pltpu.make_async_remote_copy(
            src_ref=src,
            dst_ref=dst,
            send_sem=relay_sem.at[0, number],
            recv_sem=relay_sem.at[1, number],
            device_id=target,
            device_id_type=MESH,
        )

    def spread(name, number):
        ref = gather[name]

        @pl.loop(1, NQ)
        def _(k):
            mine = ref.at[core, q]
            remote(mine, mine, number, {"row": plane_peer(k)}).start()

    def spread_wait(name, number):
        some = gather[name].at[core, 0 : NQ - 1]
        remote(some, some, number, {"row": q * 2 + other}).wait_recv()

    def share(ref, number):
        half = ref.at[core]
        remote(half, half, number, {"row": q * 2 + other}).start()

    def share_wait(ref, number):
        half = ref.at[other]
        remote(half, half, number, {"row": q * 2 + other}).wait_recv()

    def ring(src, dst, number, target):
        return pltpu.make_async_remote_copy(
            src_ref=src,
            dst_ref=dst,
            send_sem=ring_sem.at[0, number],
            recv_sem=ring_sem.at[1, number],
            device_id={"col": target},
            device_id_type=MESH,
        )

    def reduce_start(source, t, number):
        slab, landing = slabs[number], sums[number]
        have = min(4, 2**t) * 32
        for g in range(GROUPS[t]):
            part = source[g * 128 : g * 128 + have].astype(BF)
            cut = jnp.dot(perm[:, :have], part, preferred_element_type=F32).astype(BF)
            slab[:, g * GROUP : (g + 1) * GROUP] = cut.reshape(NC, GROUP, 256)

        @pl.loop(1, NC)
        def _(k):
            to = (col + k) % NC
            ring(slab.at[to], landing.at[col], number, to).start()

        landing[col] = slab[col]

    def reduce_wait(number):
        some = sums[number].at[0 : NC - 1]
        ring(some, some, number, (col + 1) % NC).wait_recv()

    def reduced(number, g):
        landing = sums[number]
        at = slice(g * GROUP, (g + 1) * GROUP)
        total = landing[0, at].astype(F32)
        for k in range(1, NC):
            total = total + landing[k, at].astype(F32)
        return total

    def product(weights, ref, g, h, first, count, lead=None):
        at = ref.shape[2] // GROUP
        block = ref[h] if at == 1 else ref[h, :, g * GROUP : (g + 1) * GROUP]
        wg = g if weights.shape[0] > 1 else 0
        return jnp.dot(
            weights[wg, h, first : first + count],
            block.reshape(NQ * GROUP, 256),
            preferred_element_type=F32,
        )

    def add_forward(t, g, h, ref, block, entry, start):
        target, at, count = entry
        weights = fw[t][g, h, at : at + count]
        value = jnp.dot(weights, block(ref, h), preferred_element_type=F32)
        if target < 0:
            base = g * 128
            if start:
                acc[t][base : base + count] = value
            else:
                acc[t][base : base + count] += value
        else:
            first = ((4 * g) >> (t - target)) * 32
            pend[target][first : first + count] += value

    def add_backward(t, g, h, ref, block, entry):
        s, at, count = entry
        weights = bw[t][g, h, at : at + count]
        value = jnp.dot(weights, block(ref, h), preferred_element_type=F32)
        first = g * 128 * 2 ** (s - t)
        acc[s][first : first + count] -= value

    def block_of(g):
        def block(ref, h):
            return ref[h, :, g * GROUP : (g + 1) * GROUP].reshape(NQ * GROUP, 256)

        return block

    def block_all(ref, h):
        return ref[h].reshape(NQ * GROUP, 256)

    for load in loads[:1]:
        load.wait()
    for t in range(4, 0, -1):
        for hop in range(t):
            mask(lw, out_row, t, hop)
    loads[2].wait()
    expand_forward(4)
    pl.semaphore_wait(barrier, NQ - 1 + NC - 1 + 1)

    f4 = gather["f4"]
    for g in range(4):

        @pl.loop(1, NZ)
        def _(k):
            mine = f4.at[g, core, q]
            remote(mine, mine, 3 * g, {"row": (x * NZ + (z + k) % NZ) * 2 + core}).start()

    expand_forward(3)
    expand_forward(2)
    for g in range(4):
        some = f4.at[g, core, 0 : NZ - 1]
        remote(some, some, 3 * g, {"row": q * 2 + other}).wait_recv()

        @pl.loop(1, NX)
        def _(k):
            line = f4.at[g, core, pl.ds(x * NZ, NZ)]
            remote(line, line, 3 * g + 1, {"row": (((x + k) % NX) * NZ + z) * 2 + core}).start()

    expand_forward(1)
    expand_forward(0)
    for g in range(4):
        some = f4.at[g, core, 0 : NQ - NZ]
        remote(some, some, 3 * g + 1, {"row": q * 2 + other}).wait_recv()
        share(f4.at[g], 3 * g + 2)
        add_forward(4, g, core, f4.at[g], block_all, FROWS[4][0][0], True)
        if g > 0:
            share_wait(f4.at[g - 1], 3 * (g - 1) + 2)
            add_forward(4, g - 1, other, f4.at[g - 1], block_all, FROWS[4][0][0], False)
    share_wait(f4.at[3], 11)
    add_forward(4, 3, other, f4.at[3], block_all, FROWS[4][0][0], False)
    reduce_start(pend[3], 3, 0)
    for g in range(4):
        for entry in FROWS[4][0][1:]:
            add_forward(4, g, core, f4.at[g], block_all, entry, True)
            add_forward(4, g, other, f4.at[g], block_all, entry, False)
    loads[1].wait()

    number = 12
    for t in range(3, -1, -1):
        name = f"f{t}"
        ref = gather[name]
        reduce_wait(3 - t)
        for g in range(GROUPS[t]):
            y = rs_ref[piece(t, g)].astype(F32) - reduced(3 - t, g)
            ref[core, q, g * GROUP : (g + 1) * GROUP] = (valid(t, g) * y).astype(BF)
        spread(name, number)
        if t == 3:
            for s in range(1, LEVELS):
                for hop in range(s):
                    mask(uw, in_row, s, hop)
            expand_backward(0)
        else:
            expand_backward(3 - t)
        spread_wait(name, number)
        share(ref, number + 1)
        for g in range(GROUPS[t]):
            add_forward(t, g, core, ref, block_of(g), FROWS[t][0][0], True)
        share_wait(ref, number + 1)
        for g in range(GROUPS[t]):
            add_forward(t, g, other, ref, block_of(g), FROWS[t][0][0], False)
        if t > 0:
            reduce_start(pend[t - 1], t - 1, 4 - t)
            for g in range(GROUPS[t]):
                for entry in FROWS[t][0][1:]:
                    add_forward(t, g, core, ref, block_of(g), entry, True)
                    add_forward(t, g, other, ref, block_of(g), entry, False)
        else:
            reduce_start(acc[0], 0, 4)
        number += 2

    for t in range(LEVELS):
        name = f"b{t}"
        reduce_wait(4 + t)
        for g in range(GROUPS[t]):
            solved = (valid(t, g) * reduced(4 + t, g)).astype(BF)
            out_ref[piece(t, g)] = solved
            if t < 4:
                gather[name][core, q, g * GROUP : (g + 1) * GROUP] = solved
        if t == 4:
            break
        ref = gather[name]
        spread(name, number)
        spread_wait(name, number)
        share(ref, number + 1)
        for g in range(GROUPS[t]):
            add_backward(t, g, core, ref, block_of(g), BROWS[t][0][0])
        share_wait(ref, number + 1)
        for g in range(GROUPS[t]):
            add_backward(t, g, other, ref, block_of(g), BROWS[t][0][0])
        reduce_start(acc[t + 1], t + 1, 5 + t)
        for g in range(GROUPS[t]):
            for entry in BROWS[t][0][1:]:
                add_backward(t, g, core, ref, block_of(g), entry)
                add_backward(t, g, other, ref, block_of(g), entry)
        number += 2

    for g in range(4):
        sent = f4.at[g, core, 0 : NZ - 1]
        remote(sent, sent, 3 * g, {"row": q * 2 + other}).wait_send()
        sent = f4.at[g, core, 0 : NQ - NZ]
        remote(sent, sent, 3 * g + 1, {"row": q * 2 + other}).wait_send()
        sent = f4.at[g, core]
        remote(sent, sent, 3 * g + 2, {"row": q * 2 + other}).wait_send()
    number = 12
    for name in ("f3", "f2", "f1", "f0", "b0", "b1", "b2", "b3"):
        sent = gather[name].at[core, 0 : NQ - 1]
        remote(sent, sent, number, {"row": q * 2 + other}).wait_send()
        sent = gather[name].at[core]
        remote(sent, sent, number + 1, {"row": q * 2 + other}).wait_send()
        number += 2
    for i in range(9):
        sent = sums[i].at[0 : NC - 1]
        ring(sent, sent, i, (col + 1) % NC).wait_send()


def scratch_shapes():
    gather = {"f4": pltpu.VMEM((4, 2, NQ, GROUP, 256), BF)}
    for t in range(4):
        for way in "fb":
            gather[f"{way}{t}"] = pltpu.VMEM((2, NQ, GROUP * GROUPS[t], 256), BF)
    order = [3, 2, 1, 0, 0, 1, 2, 3, 4]
    return {
        "lw": pltpu.VMEM((98, 32, 256), BF),
        "uw": pltpu.VMEM((98, 32, 256), BF),
        "dw": pltpu.VMEM((31, 32, 256), BF),
        "sel": pltpu.VMEM((2, 1024, 512), BF),
        "perm": pltpu.VMEM((128, 128), BF),
        "fw": [pltpu.VMEM((GROUPS[t], 2, FROWS[t][1], 512), BF) for t in range(5)],
        "bw": [pltpu.VMEM((GROUPS[t], 2, BROWS[t][1], 512), BF) for t in range(4)],
        "pend": [pltpu.VMEM((32 * 2**t, 256), F32) for t in range(4)],
        "acc": [pltpu.VMEM((32 * 2**t, 256), F32) for t in range(5)],
        "gather": gather,
        "slabs": [pltpu.VMEM((NC, GROUP * GROUPS[t], 256), BF) for t in order],
        "sums": [pltpu.VMEM((NC, GROUP * GROUPS[t], 256), BF) for t in order],
        "relay_sem": pltpu.SemaphoreType.DMA((2, 28)),
        "ring_sem": pltpu.SemaphoreType.DMA((2, 9)),
        "load_sem": pltpu.SemaphoreType.DMA((3,)),
    }


def shards(right_side, lower_blocks, upper_blocks, pivot_inverse, widths, first_row):
    zero = jnp.zeros((3, 4, 256), BF)
    padded = jnp.concatenate(
        [
            right_side[15:31],
            right_side[7:15],
            right_side[3:7],
            right_side[1:3],
            zero[:2],
            right_side[0:1],
            zero,
        ],
        axis=0,
    ).reshape(NGROUP * GROUP, 256)
    vmem = pl.BlockSpec(memory_space=pltpu.VMEM)
    smem = pl.BlockSpec(memory_space=pltpu.SMEM)
    hbm = pl.BlockSpec(memory_space=pl.ANY)
    shapes = scratch_shapes()
    leaves, tree = jax.tree.flatten(shapes)

    def body(*refs):
        kernel(*refs[:7], jax.tree.unflatten(tree, refs[7:]))

    answer = pl.pallas_call(
        body,
        out_shape=jax.ShapeDtypeStruct((NGROUP * GROUP, 256), BF),
        in_specs=[vmem, smem, smem, hbm, hbm, hbm],
        out_specs=vmem,
        scratch_shapes=leaves,
        compiler_params=pltpu.CompilerParams(
            collective_id=1, has_side_effects=True, vmem_limit_bytes=56 * 1024 * 1024
        ),
        name="tree_solve",
    )(padded, widths, first_row, lower_blocks, upper_blocks, pivot_inverse)
    nodes = answer.reshape(NGROUP * 4, 4, 256)
    return jnp.concatenate(
        [nodes[32:33], nodes[28:30], nodes[24:28], nodes[16:24], nodes[0:16]], axis=0
    )


def solution(mesh):
    in_specs = (
        P(None, ("row", "col"), None),
        P(None, "row", "col"),
        P(None, "row", "col"),
        P(None, "row", "col"),
        P(),
        P(),
    )
    out_specs = P(None, ("row", "col"), None)
    return jax.shard_map(shards, mesh=mesh, in_specs=in_specs, out_specs=out_specs, check_vma=False)
```

time: 1090 us -> 209 us (0.19)
  waiting for transfers between devices: 681 us -> 0 us
  blocking collectives: 338 us -> 0 us
  Pallas kernels: 0 us -> 197 us
  matrix products: 22.5 us -> 0 us
  between operations: 14.5 us -> 0.04 us
  other arithmetic: 11.7 us -> 0 us
    unnamed x16 -> x0, waiting for transfers between devices: 333 us -> none
    all_gather x6 -> x0, blocking collectives: 316 us -> none  [solve_all(): spread = lax.all_gather(solved, 'row', axis=1, tiled=True)]
    all_gather x3 -> x0, waiting for transfers between devices: 259 us -> none  [solve_all(): spread = lax.all_gather(solved, 'row', axis=1, tiled=True)]
    pallas_call x0 -> x1, Pallas kernels: none -> 197 us  [shards(): pl.pallas_call(body, out_shape=jax.ShapeDtypeStruct((NGROUP * GROUP, 256)...]
    reduce_scatter x3 -> x0, waiting for transfers between devices: 89 us -> none  [the longest x2 58.5 us: solve_all(): lax.psum_scatter(behind[tree_level], 'col', scatter_dimension=1, tiled=True)]
    dot_general x21 -> x0, matrix products: 22.5 us -> none  [multiply(): jnp.einsum('nij,njr->nir', blocks, vectors, preferred_element_type=jnp.fl...]
    unnamed x1 -> x0, blocking collectives: 21.8 us -> none
  transfers between devices with their start and end apart: 11 -> 0, of which waited for: 11 -> 0; matrix products, arithmetic and copies ran while one was open for 2% -> 0% of each run, Pallas kernels for 0% -> 0%
where the time goes in v1:
time: 209 us; the launch traced here: 207 us
  Pallas kernels  197 us (94%)
  local copies, waits for them, and re-layouts  10.5 us (5%)
    pallas_call x1, Pallas kernels, shards(): pl.pallas_call(body, out_shape=jax.ShapeDtypeStruct((NGROUP * GROUP, 256)...  197 us
    unnamed x13, local copies, waits for them, and re-layouts  6.29 us

profile of v1, /device:TPU:1, one launch (start us, length us, event | category | flops | bytes accessed | tf_op | source)
XLA Modules:
  0.0 207.4 jit_solution(11120695676686569805)
XLA Ops:
  0.0 1.4 copy.7.refs_2_
  1.4 0.8 slice_dynamic-update-slice_fusion
  2.1 0.7 constant_dynamic-update-slice_fusion.5
  2.9 0.7 constant_dynamic-update-slice_fusion.4
  3.6 0.7 constant_dynamic-update-slice_fusion.3
  4.3 0.7 constant_dynamic-update-slice_fusion.1
  5.0 0.6 reshape.9.refs_0_
  5.6 196.9 %tree_solve.1 = bf16[144,256]{1,0:T(8,128)(2,1)} custom-call(bf16[144,256]{1,0:T(8,128)(2,1)} %reshape.9.refs_0_, s32[31]{0:T(128)} %refs_1_.1, s32[31,4]{1,0:T(8,128)} %copy.7.refs_2_, bf16[98,32,256]{2,1,0:T(8,128)(2,1)} %refs_3_.1, bf16[98,32,256]{2,1,0:T(8,128)(2,1)} %refs_4_.1, bf16[31,32,256]{2,1,0:T(8,128)(2,1)} %refs_5_.1), custom_call_target="tpu_custom_call" | custom-call | tf_op jit(solution)/shard_map/tree_solve/pallas_call | solution.py:467
  202.5 0.7 slice.56
  203.2 0.7 slice.58
  203.9 0.7 slice.60
  204.7 0.8 slice.62
  205.4 0.7 constant_dynamic-update-slice_fusion.10
  206.1 0.0 copy-start
  206.2 0.6 copy-done
  206.8 0.6 constant_dynamic-update-slice_fusion.6
  (9 shorter events, 0.1 us)
Async XLA Ops:
  206.1 0.6 copy-start

commit v2 on v1

v2 whole, which is shorter than its diff:
```python
import functools

import jax
import jax.numpy as jnp
from jax import lax
from jax.experimental import pallas as pl
from jax.experimental.pallas import tpu as pltpu
from jax.sharding import PartitionSpec as P

MESH = pl.DeviceIdType.MESH
BF = jnp.bfloat16
F32 = jnp.float32
LEVELS = 5
NX, NZ, NC = 4, 8, 8
NQ = NX * NZ
TOP = 2
GROUPS = [1, 1, 1, 2, 4]
GBASE = [7, 7, 6, 4, 0]
NGROUP = 8
GROUP = 16


def block_offsets():
    offsets = {}
    running = 0
    for tree_level in range(1, LEVELS):
        for hop_up in range(tree_level):
            offsets[tree_level, hop_up] = running
            running = running + 2**tree_level
    return offsets


OFF = block_offsets()


def forward_rows(t):
    rows, at = [], 0
    for hop in range(t):
        count = 64 if hop == 0 else 32
        rows.append((t - 1 - hop, at, count))
        at += count
    rows.append((-1, at, 128))
    return rows, at + 128


def backward_rows(t):
    rows, at = [], 0
    for s in range(t + 1, LEVELS):
        count = 32 * (2**s if t == 1 else 4 * 2 ** (s - t))
        rows.append((s, at, count))
        at += count
    return rows, at


FROWS = {t: forward_rows(t) for t in range(TOP, LEVELS)}
BROWS = {t: backward_rows(t) for t in range(1, LEVELS - 1)}
TL, TU, TD, TOPS = 0, 2, 4, 7
R3, R2, P1, P0, SPLIT, B2, B3, B4, PANEL, MPANEL, RINGS = range(11)


def kernel(rs_ref, widths_ref, first_ref, l_hbm, u_hbm, d_hbm, out_ref, scratch):
    row = lax.axis_index("row")
    col = lax.axis_index("col")
    x, z, core = row // 16, (row // 2) % 8, row % 2
    q = x * NZ + z
    other = 1 - core
    lw, uw, dw, sel, perm = (scratch[n] for n in ("lw", "uw", "dw", "sel", "perm"))
    fw, bw, pend, acc = (scratch[n] for n in ("fw", "bw", "pend", "acc"))
    rows_in, rows_out = scratch["rows_in"], scratch["rows_out"]
    gather, relay_sem, load_sem = scratch["gather"], scratch["relay_sem"], scratch["load_sem"]
    slabs, sums, ring_sem = scratch["slabs"], scratch["sums"], scratch["ring_sem"]
    panel, mpanel, split = scratch["panel"], scratch["mpanel"], scratch["split"]
    top1, top0, wide_u = scratch["top1"], scratch["top0"], scratch["wide_u"]
    place, packed = scratch["place"], scratch["packed"]

    loads = [
        pltpu.make_async_copy(src, dst, load_sem.at[i])
        for i, (src, dst) in enumerate(((l_hbm, lw), (u_hbm, uw), (d_hbm, dw)))
    ]
    for load in loads:
        load.start()

    barrier = pltpu.get_barrier_semaphore()

    def plane_peer(k):
        px, pz = (x + k // NZ) % NX, (z + k % NZ) % NZ
        return (px * NZ + pz) * 2 + core

    def signal(target):
        pl.semaphore_signal(barrier, inc=1, device_id=target, device_id_type=MESH)

    @pl.loop(1, NQ)
    def _(k):
        signal({"row": plane_peer(k)})

    @pl.loop(1, NC)
    def _(k):
        signal({"col": (col + k) % NC})

    signal({"row": q * 2 + other})

    def iota(shape, dim):
        return lax.broadcasted_iota(jnp.int32, shape, dim)

    def table(hit):
        return hit.astype(F32).astype(BF)

    def heap_row(r):
        s = r // 4
        n = jnp.where(s < 16, s + 15, jnp.where(s < 24, s - 9, jnp.where(s < 28, s - 21, s - 28)))
        return n * 4 + r % 4

    rows_out[...] = jnp.zeros_like(rows_out)
    rows_out[0:124] = rs_ref[...]
    order = table(iota((128, 128), 1) == heap_row(iota((128, 128), 0)))
    rows_in[...] = jnp.dot(order, rows_out[...], preferred_element_type=F32).astype(BF)

    row16 = iota((GROUP, 256), 0)
    own_row = row * 32 + col * 4 + row16 % 4

    def valid(t, g):
        limit = jnp.zeros((GROUP, 256), jnp.int32)
        for j in range(4):
            limit = jnp.where(row16 // 4 == j, widths_ref[2**t - 1 + 4 * g + j], limit)
        return (own_row < limit).astype(F32)

    def piece(t, g):
        at = (GBASE[t] + g) * GROUP
        return slice(at, at + GROUP)

    for g in range(4):
        y = valid(4, g) * rows_in[piece(4, g)].astype(F32)
        gather["f4"][g, core, q] = y.astype(BF)

    @pl.loop(0, 2)
    def _(h):
        @pl.loop(0, 8)
        def _(b):
            r = iota((128, 512), 0) + b * 128
            s = iota((128, 512), 1)
            p = (r % 256) // 4
            target = (p // 2) * 16 + (r // 256) * 4 + r % 4
            hit = jnp.logical_and(s == target, p % 2 == h)
            sel[h, pl.ds(pl.multiple_of(b * 128, 128), 128)] = table(hit)

    r, s = iota((128, 128), 0), iota((128, 128), 1)
    perm[...] = table(s == ((r // 4) % 4) * 32 + (r // 16) * 4 + r % 4)

    out_row = row * 32 + iota((32, 256), 0)
    lane = iota((32, 256), 1)
    in_row = (lane // 4) * 32 + col * 4 + lane % 4

    def mask(ref, index, t, hop):
        @pl.loop(0, 2**t)
        def _(n):
            keep = table(index >= first_ref[2**t - 1 + n, hop])
            ref[OFF[t, hop] + n] = ref[OFF[t, hop] + n] * keep

    def stack(ref, base, groups, members):
        return jnp.concatenate(
            [
                jnp.concatenate([ref[base + 4 * g + j] for j in members], axis=1)
                for g in range(groups)
            ],
            axis=0,
        )

    def expand(left, h, first, last):
        part = sel[h, first * 256 : last * 256]
        return jnp.dot(left, part, preferred_element_type=F32)

    def expand_forward(t):
        groups = GROUPS[t]
        for target, at, count in FROWS[t][0]:
            if target >= 0:
                hop = t - 1 - target
                halves = count // 32
                per = 4 // halves
                jobs = [
                    (lw, OFF[t, hop], at + 32 * v, [v * per + w for w in range(per)])
                    for v in range(halves)
                ]
            else:
                jobs = [(dw, 2**t - 1, at + 32 * j, [j]) for j in range(4)]
            for ref, base, first, members in jobs:
                left = stack(ref, base, groups, members)

                @pl.loop(0, 2)
                def _(h):
                    wide = expand(left, h, members[0], members[-1] + 1).astype(BF)
                    for g in range(groups):
                        fw[t][g, h, first : first + 32] = wide[g * 32 : (g + 1) * 32]

    def uppers(s, hop, first, count):
        base = OFF[s, hop] + first
        return uw[base : base + count].reshape(count * 32, 256)

    def expand_backward(t):
        for s, at, count in BROWS[t][0]:
            if t == 1:
                each = 2 ** (s - 1)
                for a in range(2):
                    root = uppers(s, s - 1, a * each, each)
                    parent = uppers(s, s - 2, a * each, each)
                    first = at + a * each * 32

                    @pl.loop(0, 2)
                    def _(h):
                        wide = expand(root, h, 0, 1) + expand(parent, h, 1 + a, 2 + a)
                        bw[t][0, h, first : first + each * 32] = wide.astype(BF)

                continue
            each = 2 ** (s - t)
            for g in range(GROUPS[t]):
                for j in range(4):
                    left = uppers(s, s - 1 - t, (4 * g + j) * each, each)
                    first = at + j * each * 32

                    @pl.loop(0, 2)
                    def _(h):
                        wide = expand(left, h, j, j + 1).astype(BF)
                        bw[t][g, h, first : first + each * 32] = wide

    def remote(src, dst, number, target):
        return pltpu.make_async_remote_copy(
            src_ref=src,
            dst_ref=dst,
            send_sem=relay_sem.at[0, number],
            recv_sem=relay_sem.at[1, number],
            device_id=target,
            device_id_type=MESH,
        )

    def spread(ref, number):
        @pl.loop(1, NQ)
        def _(k):
            mine = ref.at[core, q]
            remote(mine, mine, number, {"row": plane_peer(k)}).start()

    def spread_wait(ref, number):
        some = ref.at[core, 0 : NQ - 1]
        remote(some, some, number, {"row": q * 2 + other}).wait_recv()

    def share(ref, number):
        half = ref.at[core]
        remote(half, half, number, {"row": q * 2 + other}).start()

    def share_wait(ref, number):
        half = ref.at[other]
        remote(half, half, number, {"row": q * 2 + other}).wait_recv()

    def ring(src, dst, number, target):
        return pltpu.make_async_remote_copy(
            src_ref=src,
            dst_ref=dst,
            send_sem=ring_sem.at[0, number],
            recv_sem=ring_sem.at[1, number],
            device_id={"col": target},
            device_id_type=MESH,
        )

    def ring_all(landing, number):
        @pl.loop(1, NC)
        def _(k):
            mine = landing.at[col]
            ring(mine, mine, number, (col + k) % NC).start()

    def ring_wait(landing, number):
        some = landing.at[0 : NC - 1]
        ring(some, some, number, (col + 1) % NC).wait_recv()

    def reduce_start(source, t, number):
        for g in range(GROUPS[t]):
            part = source[g * 128 : (g + 1) * 128].astype(BF)
            cut = jnp.dot(perm[...], part, preferred_element_type=F32).astype(BF)
            slabs[number][:, g * GROUP : (g + 1) * GROUP] = cut.reshape(NC, GROUP, 256)
        reduce_send(number)

    def reduce_send(number):
        slab, landing = slabs[number], sums[number]

        @pl.loop(1, NC)
        def _(k):
            to = (col + k) % NC
            ring(slab.at[to], landing.at[col], number, to).start()

        landing[col] = slab[col]

    def reduced(number, at):
        landing = sums[number]
        total = landing[0, at].astype(F32)
        for k in range(1, NC):
            total = total + landing[k, at].astype(F32)
        return total

    lane_block = iota((8, 128), 1) // 32

    def pack(blocks):
        total = jnp.where(lane_block == 0, blocks[0], 0.0)
        for b in range(1, 4):
            total = total + jnp.where(lane_block == b, blocks[b], 0.0)
        return total

    def split_start(t, number):
        kind = slabs[number].dtype
        for u in range(2):
            for w in range(4):
                cut = []
                for n in range(2**t):
                    blocks = [
                        pend[t][n * 32 + b * 8 : n * 32 + b * 8 + 8, u * 128 : u * 128 + 128]
                        for b in range(4)
                    ]
                    blocks = [
                        v if b == w else pltpu.roll(v, ((b - w) * 32) % 128, 1)
                        for b, v in enumerate(blocks)
                    ]
                    cut.append(pack(blocks))
                whole = cut[0] if t == 0 else jnp.concatenate(cut, axis=0)
                slabs[number][4 * u + w] = whole.astype(kind)
        reduce_send(number)

    def valid_top(n):
        r = row * 32 + lane_block * 8 + iota((8, 128), 0)
        return (r < widths_ref[n]).astype(F32)

    def fold(wide):
        lanes = iota((32, 128), 1) // 32
        total = jnp.where(lanes == 0, wide[0:32], 0.0)
        for b in range(1, 4):
            total = total + jnp.where(lanes == b, wide[b * 32 : b * 32 + 32], 0.0)
        total = total + pltpu.roll(total, 64, 1)
        total = total + pltpu.roll(total, 32, 1)
        return pack([total[b * 8 : b * 8 + 8] for b in range(4)])

    def top_product(weights, ref, first, count):
        near = ref[core].reshape(NQ * GROUP, 128)
        far = ref[other].reshape(NQ * GROUP, 128)
        rows = slice(first, first + count)
        return jnp.dot(weights[core, rows], near, preferred_element_type=F32) + jnp.dot(
            weights[other, rows], far, preferred_element_type=F32
        )

    def panels(ref, index, b):
        return jnp.concatenate([ref[2 * b, index], ref[2 * b + 1, index]], axis=1)

    def block_of(ref, h, g):
        if ref.shape[2] == GROUP:
            return ref[h].reshape(NQ * GROUP, 256)
        return ref[h, :, g * GROUP : (g + 1) * GROUP].reshape(NQ * GROUP, 256)

    def add_forward(t, g, h, ref, entry, start):
        target, at, count = entry
        weights = fw[t][g, h, at : at + count]
        value = jnp.dot(weights, block_of(ref, h, g), preferred_element_type=F32)
        if target < 0:
            base = g * 128
            if start:
                acc[t][base : base + count] = value
            else:
                acc[t][base : base + count] += value
        else:
            first = ((4 * g) >> (t - target)) * 32
            pend[target][first : first + count] += value

    def add_backward(t, g, h, ref, entry):
        s, at, count = entry
        weights = bw[t][g, h, at : at + count]
        value = jnp.dot(weights, block_of(ref, h, g), preferred_element_type=F32)
        first = g * 128 * 2 ** (s - t)
        acc[s][first : first + count] -= value

    for load in loads:
        load.wait()
    mask(lw, out_row, 1, 0)
    mask(uw, in_row, 1, 0)
    for n in range(2):
        panel[col, TL + n] = lw[OFF[1, 0] + n]
        panel[col, TU + n] = uw[OFF[1, 0] + n]
    d0 = gather["d0"]
    inside = dw[0] * table(out_row < widths_ref[0])
    panel[col, TD] = inside
    for i in range(2):
        d0[i, core, q] = inside[i * GROUP : (i + 1) * GROUP]
    for n in range(1, 3):
        panel[col, TD + n] = dw[n]
    for t in range(4, 1, -1):
        for hop in range(t):
            mask(lw, out_row, t, hop)

    e, f = iota((96, GROUP), 0), iota((96, GROUP), 1)
    expanded = table(jnp.logical_and(e // 32 == f // 4, e % 32 == col * 4 + f % 4))
    begun = -jnp.dot(expanded, rows_in[piece(0, 0)], preferred_element_type=F32)
    pend[0][...] = begun[0:32]
    pend[1][...] = begun[32:96]
    for t in range(2, 4):
        pend[t][...] = jnp.zeros_like(pend[t])
    expand_forward(4)
    pl.semaphore_wait(barrier, NQ - 1 + NC - 1 + 1)

    f4 = gather["f4"]
    for g in range(4):

        @pl.loop(1, NZ)
        def _(k):
            mine = f4.at[g, core, q]
            remote(mine, mine, 3 * g, {"row": (x * NZ + (z + k) % NZ) * 2 + core}).start()

    ring_all(panel, PANEL)
    expand_forward(3)
    expand_forward(2)
    for g in range(4):
        some = f4.at[g, core, 0 : NZ - 1]
        remote(some, some, 3 * g, {"row": q * 2 + other}).wait_recv()

        @pl.loop(1, NX)
        def _(k):
            line = f4.at[g, core, pl.ds(x * NZ, NZ)]
            remote(line, line, 3 * g + 1, {"row": (((x + k) % NX) * NZ + z) * 2 + core}).start()

    for s in range(1, LEVELS):
        for hop in range(s):
            if s > 1:
                mask(uw, in_row, s, hop)
    @pl.loop(0, 8)
    def _(b):
        r, s = iota((128, 256), 0), iota((128, 256), 1)
        hit = jnp.logical_and(r // 32 == col // 2, s == b * 32 + r % 32)
        place[pl.ds(pl.multiple_of(b * 128, 128), 128)] = table(hit)

    parents = FROWS[4][0][0]
    for g in range(4):
        some = f4.at[g, core, 0 : NQ - NZ]
        remote(some, some, 3 * g + 1, {"row": q * 2 + other}).wait_recv()
        share(f4.at[g], 3 * g + 2)
        add_forward(4, g, core, f4.at[g], parents, True)
        if g > 0:
            share_wait(f4.at[g - 1], 3 * (g - 1) + 2)
            add_forward(4, g - 1, other, f4.at[g - 1], parents, False)
    share_wait(f4.at[3], 11)
    add_forward(4, 3, other, f4.at[3], parents, False)
    reduce_start(pend[3], 3, R3)
    spread(d0.at[0], 12)
    for g in range(4):
        for entry in FROWS[4][0][1:]:
            add_forward(4, g, core, f4.at[g], entry, True)
            add_forward(4, g, other, f4.at[g], entry, False)

    for t, number, ringed in ((3, 14, R3), (2, 16, R2)):
        ref = gather[f"f{t}"]
        ring_wait(sums[ringed], ringed)
        for g in range(GROUPS[t]):
            at = slice(g * GROUP, (g + 1) * GROUP)
            y = rows_in[piece(t, g)].astype(F32) - reduced(ringed, at)
            ref[core, q, at] = (valid(t, g) * y).astype(BF)
        spread(ref, number)
        if t == 3:
            ring_wait(panel, PANEL)
            for g in range(2):
                for n in range(2):
                    left = jnp.concatenate([panel[4 * g + j, TU + n] for j in range(4)], axis=1)

                    @pl.loop(0, 2)
                    def _(h):
                        wide_u[g, h, n * 32 : n * 32 + 32] = expand(left, h, 0, 4).astype(BF)

            left = jnp.concatenate(
                [
                    jnp.concatenate([panels(panel, TL, b), panels(panel, TL + 1, b)], axis=1)
                    for b in range(4)
                ],
                axis=0,
            )

            @pl.loop(0, 2)
            def _(h):
                top1[h, 0:128] = expand(left, h, 0, 4).astype(BF)

            for n in range(3):
                left = jnp.concatenate([panels(panel, TD + n, b) for b in range(4)], axis=0)

                @pl.loop(0, 2)
                def _(h):
                    if n == 0:
                        top0[h, 0:128] = expand(left, h, 0, 2).astype(BF)
                    else:
                        wide = expand(left, h, 2 * n - 2, 2 * n).astype(BF)
                        top1[h, n * 128 : n * 128 + 128] = wide

        else:
            expand_backward(1)
        spread_wait(ref, number)
        share(ref, number + 1)
        parents = FROWS[t][0][0]
        for g in range(GROUPS[t]):
            add_forward(t, g, core, ref, parents, True)
        share_wait(ref, number + 1)
        for g in range(GROUPS[t]):
            add_forward(t, g, other, ref, parents, False)
        if t == 3:
            reduce_start(pend[2], 2, R2)
            spread_wait(d0.at[0], 12)
            share(d0.at[0], 13)
            spread(d0.at[1], 18)
        else:
            split_start(1, P1)
        for g in range(GROUPS[t]):
            for entry in FROWS[t][0][1:]:
                add_forward(t, g, core, ref, entry, True)
                add_forward(t, g, other, ref, entry, False)

    split_start(0, P0)
    spread_wait(d0.at[1], 18)
    share(d0.at[1], 19)
    y1 = gather["y1"]
    ring_wait(sums[P1], P1)
    solved = -reduced(P1, slice(0, GROUP))
    for n in range(2):
        solved_n = valid_top(1 + n) * solved[n * 8 : n * 8 + 8]
        packed[n * 8 : n * 8 + 8] = solved_n
    y1[core, q] = packed[...].astype(BF)
    spread(y1, 20)
    share_wait(d0.at[0], 13)
    share_wait(d0.at[1], 19)
    product = jnp.zeros((64, 256), F32)
    for g in range(2):
        for h in range(2):
            product = product + jnp.dot(
                wide_u[g, h], d0[g, h].reshape(NQ * GROUP, 256), preferred_element_type=F32
            )
    mpanel[col] = product.astype(BF).reshape(2, 32, 256)
    ring_all(mpanel, MPANEL)
    expand_backward(2)
    ring_wait(sums[P0], P0)
    spread_wait(y1, 20)
    share(y1, 21)
    share_wait(y1, 21)
    y0 = -reduced(P0, slice(0, 8)) - fold(top_product(top1, y1, 0, 128))
    y0 = valid_top(0) * y0
    ref = gather["y0"]
    packed[0:8] = y0
    packed[8:16] = jnp.zeros((8, 128), F32)
    ref[core, q] = packed[...].astype(BF)
    spread(ref, 22)
    wide = top_product(top1, y1, 128, 256)
    scaled = [fold(wide[n * 128 : n * 128 + 128]) for n in range(2)]
    ring_wait(mpanel, MPANEL)
    for n in range(2):
        left = jnp.concatenate([panels(mpanel, n, b) for b in range(4)], axis=0)

        @pl.loop(0, 2)
        def _(h):
            wide = expand(left, h, 0, 2).astype(BF)
            top0[h, 128 + n * 128 : 256 + n * 128] = wide

    expand_backward(3)
    spread_wait(ref, 22)
    share(ref, 23)
    share_wait(ref, 23)
    wide = top_product(top0, ref, 0, 384)
    split[col, 0:8] = (valid_top(0) * fold(wide[0:128])).astype(BF)
    for n in range(2):
        s1 = scaled[n] - fold(wide[128 + n * 128 : 256 + n * 128])
        packed[n * 8 : n * 8 + 8] = valid_top(1 + n) * s1
    split[col, 8:24] = packed[...].astype(BF)
    split[col, 24:32] = jnp.zeros((8, 128), BF)
    ring_all(split, SPLIT)
    e, f = iota((GROUP, 32), 0), iota((GROUP, 32), 1)
    rows = table(f == (e // 4) * 8 + (col % 2) * 4 + e % 4)
    ring_wait(split, SPLIT)
    side = jnp.concatenate([split[k] for k in range(NC)], axis=1)
    side = jnp.dot(side, place[...], preferred_element_type=F32).astype(BF)
    solved = jnp.dot(rows, side, preferred_element_type=F32).astype(BF)
    rows_out[piece(0, 0)] = solved

    gather["b1"][core, q] = solved
    for t, number, ringed in ((1, 24, None), (2, 26, B2), (3, 28, B3), (4, None, B4)):
        if t > 1:
            ring_wait(sums[ringed], ringed)
            for g in range(GROUPS[t]):
                at = slice(g * GROUP, (g + 1) * GROUP)
                solved = (valid(t, g) * reduced(ringed, at)).astype(BF)
                rows_out[piece(t, g)] = solved
                if t < 4:
                    gather[f"b{t}"][core, q, at] = solved
        if t == 4:
            break
        ref = gather[f"b{t}"]
        spread(ref, number)
        spread_wait(ref, number)
        share(ref, number + 1)
        children = BROWS[t][0][0]
        for g in range(GROUPS[t]):
            add_backward(t, g, core, ref, children)
        share_wait(ref, number + 1)
        for g in range(GROUPS[t]):
            add_backward(t, g, other, ref, children)
        reduce_start(acc[t + 1], t + 1, {1: B2, 2: B3, 3: B4}[t])
        for g in range(GROUPS[t]):
            for entry in BROWS[t][0][1:]:
                add_backward(t, g, core, ref, entry)
                add_backward(t, g, other, ref, entry)

    order = table(iota((128, 128), 0) == heap_row(iota((128, 128), 1)))
    answer = jnp.dot(order, rows_out[...], preferred_element_type=F32).astype(BF)
    out_ref[...] = answer[0:124]

    for g in range(4):
        sent = f4.at[g, core, 0 : NZ - 1]
        remote(sent, sent, 3 * g, {"row": q * 2 + other}).wait_send()
        sent = f4.at[g, core, 0 : NQ - NZ]
        remote(sent, sent, 3 * g + 1, {"row": q * 2 + other}).wait_send()
        sent = f4.at[g, core]
        remote(sent, sent, 3 * g + 2, {"row": q * 2 + other}).wait_send()
    for ref, first, second in (
        (d0.at[0], 12, 13),
        (gather["f3"], 14, 15),
        (gather["f2"], 16, 17),
        (d0.at[1], 18, 19),
        (gather["y1"], 20, 21),
        (gather["y0"], 22, 23),
        (gather["b1"], 24, 25),
        (gather["b2"], 26, 27),
        (gather["b3"], 28, 29),
    ):
        sent = ref.at[core, 0 : NQ - 1]
        remote(sent, sent, first, {"row": q * 2 + other}).wait_send()
        sent = ref.at[core]
        remote(sent, sent, second, {"row": q * 2 + other}).wait_send()
    for number in range(RINGS):
        landing = {SPLIT: split, PANEL: panel, MPANEL: mpanel}.get(number)
        landing = sums[number] if landing is None else landing
        sent = landing.at[0 : NC - 1]
        ring(sent, sent, number, (col + 1) % NC).wait_send()


def scratch_shapes():
    gather = {
        "f4": pltpu.VMEM((4, 2, NQ, GROUP, 256), BF),
        "d0": pltpu.VMEM((2, 2, NQ, GROUP, 256), BF),
        "y1": pltpu.VMEM((2, NQ, GROUP, 128), BF),
        "y0": pltpu.VMEM((2, NQ, GROUP, 128), BF),
    }
    for name, t in (("f3", 3), ("f2", 2), ("b1", 1), ("b2", 2), ("b3", 3)):
        gather[name] = pltpu.VMEM((2, NQ, GROUP * GROUPS[t], 256), BF)
    slabs = {n: pltpu.VMEM((NC, GROUP * k, 256), BF) for n, k in ((R3, 2), (R2, 1), (B2, 1), (B3, 2), (B4, 4))}
    slabs[P1] = pltpu.VMEM((NC, GROUP, 128), BF)
    slabs[P0] = pltpu.VMEM((NC, 8, 128), F32)
    return {
        "lw": pltpu.VMEM((98, 32, 256), BF),
        "uw": pltpu.VMEM((98, 32, 256), BF),
        "dw": pltpu.VMEM((31, 32, 256), BF),
        "rows_in": pltpu.VMEM((128, 256), BF),
        "rows_out": pltpu.VMEM((128, 256), BF),
        "sel": pltpu.VMEM((2, 1024, 512), BF),
        "perm": pltpu.VMEM((128, 128), BF),
        "place": pltpu.VMEM((1024, 256), BF),
        "packed": pltpu.VMEM((GROUP, 128), F32),
        "fw": {t: pltpu.VMEM((GROUPS[t], 2, FROWS[t][1], 512), BF) for t in FROWS},
        "bw": {t: pltpu.VMEM((GROUPS[t], 2, BROWS[t][1], 512), BF) for t in BROWS},
        "top1": pltpu.VMEM((2, 384, 512), BF),
        "top0": pltpu.VMEM((2, 384, 512), BF),
        "wide_u": pltpu.VMEM((2, 2, 64, 512), BF),
        "panel": pltpu.VMEM((NC, TOPS, 32, 256), BF),
        "mpanel": pltpu.VMEM((NC, 2, 32, 256), BF),
        "split": pltpu.VMEM((NC, 32, 128), BF),
        "pend": [pltpu.VMEM((32 * 2**t, 256), F32) for t in range(4)],
        "acc": {t: pltpu.VMEM((32 * 2**t, 256), F32) for t in range(TOP, LEVELS)},
        "gather": gather,
        "slabs": slabs,
        "sums": dict(slabs),
        "relay_sem": pltpu.SemaphoreType.DMA((2, 30)),
        "ring_sem": pltpu.SemaphoreType.DMA((2, RINGS)),
        "load_sem": pltpu.SemaphoreType.DMA((3,)),
    }


def shards(right_side, lower_blocks, upper_blocks, pivot_inverse, widths, first_row):
    nodes, rows, columns = right_side.shape
    vmem = pl.BlockSpec(memory_space=pltpu.VMEM)
    smem = pl.BlockSpec(memory_space=pltpu.SMEM)
    hbm = pl.BlockSpec(memory_space=pl.ANY)
    leaves, tree = jax.tree.flatten(scratch_shapes())

    def body(*refs):
        kernel(*refs[:7], jax.tree.unflatten(tree, refs[7:]))

    answer = pl.pallas_call(
        body,
        out_shape=jax.ShapeDtypeStruct((nodes * rows, columns), BF),
        in_specs=[vmem, smem, smem, hbm, hbm, hbm],
        out_specs=vmem,
        scratch_shapes=leaves,
        compiler_params=pltpu.CompilerParams(
            collective_id=1, has_side_effects=True, vmem_limit_bytes=56 * 1024 * 1024
        ),
        name="tree_solve",
    )(
        right_side.reshape(nodes * rows, columns),
        widths,
        first_row,
        lower_blocks,
        upper_blocks,
        pivot_inverse,
    )
    return answer.reshape(nodes, rows, columns)


def solution(mesh):
    in_specs = (
        P(None, ("row", "col"), None),
        P(None, "row", "col"),
        P(None, "row", "col"),
        P(None, "row", "col"),
        P(),
        P(),
    )
    out_specs = P(None, ("row", "col"), None)
    return jax.shard_map(shards, mesh=mesh, in_specs=in_specs, out_specs=out_specs, check_vma=False)
```

time: 209 us -> 180 us (0.86)
  Pallas kernels: 197 us -> 176 us
  local copies, waits for them, and re-layouts: 10.5 us -> 4.33 us
    pallas_call x1, Pallas kernels: 197 us -> 176 us  [shards(): pl.pallas_call(body, out_shape=jax.ShapeDtypeStruct((nodes * rows, column...]
    unnamed x13 -> x1, local copies, waits for them, and re-layouts: 6.29 us -> 1.37 us
    slice x8 -> x0, local copies, waits for them, and re-layouts: 2.91 us -> none  [the longest x2 0.78 us: shards(): nodes[0:16]]
    reshape x1 -> x2, local copies, waits for them, and re-layouts: 0.64 us -> 2.96 us  [the longest x1 1.48 us: shards(): return answer.reshape(nodes, rows, columns)]
where the time goes in v2:
time: 180 us
  Pallas kernels  176 us (98%)
  local copies, waits for them, and re-layouts  4.33 us (2%)
    pallas_call x1, Pallas kernels, shards(): pl.pallas_call(body, out_shape=jax.ShapeDtypeStruct((nodes * rows, column...  176 us

profile of v2, /device:TPU:1, one launch (start us, length us, event | category | flops | bytes accessed | tf_op | source)
XLA Modules:
  0.0 180.1 jit_solution(2315459842620685083)
XLA Ops:
  0.0 1.4 copy.7.refs_2_
  1.4 1.5 reshape.6.refs_0_
  2.8 175.8 %tree_solve.1 = bf16[124,256]{1,0:T(8,128)(2,1)} custom-call(bf16[124,256]{1,0:T(8,128)(2,1)} %reshape.6.refs_0_, s32[31]{0:T(128)} %refs_1_.1, s32[31,4]{1,0:T(8,128)} %copy.7.refs_2_, bf16[98,32,256]{2,1,0:T(8,128)(2,1)} %refs_3_.1, bf16[98,32,256]{2,1,0:T(8,128)(2,1)} %refs_4_.1, bf16[31,32,256]{2,1,0:T(8,128)(2,1)} %refs_5_.1), custom_call_target="tpu_custom_call" | custom-call | tf_op jit(solution)/shard_map/tree_solve/pallas_call | solution.py:688
  178.6 1.5 reshape.7

commit v3 on v2

--- a/solution.py
+++ b/solution.py
@@ -66,7 +66,7 @@
     other = 1 - core
     lw, uw, dw, sel, perm = (scratch[n] for n in ("lw", "uw", "dw", "sel", "perm"))
     fw, bw, pend, acc = (scratch[n] for n in ("fw", "bw", "pend", "acc"))
-    rows_in, rows_out = scratch["rows_in"], scratch["rows_out"]
+    rows_in, rows_out, heap = (scratch[n] for n in ("rows_in", "rows_out", "heap"))
     gather, relay_sem, load_sem = scratch["gather"], scratch["relay_sem"], scratch["load_sem"]
     slabs, sums, ring_sem = scratch["slabs"], scratch["sums"], scratch["ring_sem"]
     panel, mpanel, split = scratch["panel"], scratch["mpanel"], scratch["split"]
@@ -82,20 +82,23 @@
 
     barrier = pltpu.get_barrier_semaphore()
 
+    def away(k, n):
+        return (n // 2 + (k + 1) // 2 * (1 - 2 * ((k + 1) % 2))) % n
+
     def plane_peer(k):
-        px, pz = (x + k // NZ) % NX, (z + k % NZ) % NZ
+        px, pz = (x + away(k % NX, NX)) % NX, (z + away(k // NX, NZ)) % NZ
         return (px * NZ + pz) * 2 + core
 
     def signal(target):
         pl.semaphore_signal(barrier, inc=1, device_id=target, device_id_type=MESH)
 
-    @pl.loop(1, NQ)
+    @pl.loop(0, NQ - 1)
     def _(k):
         signal({"row": plane_peer(k)})
 
-    @pl.loop(1, NC)
+    @pl.loop(0, NC - 1)
     def _(k):
-        signal({"col": (col + k) % NC})
+        signal({"col": (col + away(k, NC)) % NC})
 
     signal({"row": q * 2 + other})
 
@@ -110,10 +113,11 @@
         n = jnp.where(s < 16, s + 15, jnp.where(s < 24, s - 9, jnp.where(s < 28, s - 21, s - 28)))
         return n * 4 + r % 4
 
-    rows_out[...] = jnp.zeros_like(rows_out)
-    rows_out[0:124] = rs_ref[...]
+    heap[124:128] = jnp.zeros((4, 256), F32)
+    for n in range(31):
+        heap[4 * n : 4 * n + 4] = rs_ref[n].astype(F32)
     order = table(iota((128, 128), 1) == heap_row(iota((128, 128), 0)))
-    rows_in[...] = jnp.dot(order, rows_out[...], preferred_element_type=F32).astype(BF)
+    rows_in[...] = jnp.dot(order, heap[...].astype(BF), preferred_element_type=F32).astype(BF)
 
     row16 = iota((GROUP, 256), 0)
     own_row = row * 32 + col * 4 + row16 % 4
@@ -130,7 +134,7 @@
 
     for g in range(4):
         y = valid(4, g) * rows_in[piece(4, g)].astype(F32)
-        gather["f4"][g, core, q] = y.astype(BF)
+        gather["f4"][g, core, x, z] = y.astype(BF)
 
     @pl.loop(0, 2)
     def _(h):
@@ -153,7 +157,7 @@
     def mask(ref, index, t, hop):
         @pl.loop(0, 2**t)
         def _(n):
-            keep = table(index >= first_ref[2**t - 1 + n, hop])
+            keep = table(index >= first_ref[hop, 2**t - 1 + n])
             ref[OFF[t, hop] + n] = ref[OFF[t, hop] + n] * keep
 
     def stack(ref, base, groups, members):
@@ -169,9 +173,9 @@
         part = sel[h, first * 256 : last * 256]
         return jnp.dot(left, part, preferred_element_type=F32)
 
-    def expand_forward(t):
+    def expand_forward(t, entries):
         groups = GROUPS[t]
-        for target, at, count in FROWS[t][0]:
+        for target, at, count in entries:
             if target >= 0:
                 hop = t - 1 - target
                 halves = count // 32
@@ -221,6 +225,8 @@
                         wide = expand(left, h, j, j + 1).astype(BF)
                         bw[t][g, h, first : first + each * 32] = wide
 
+    leaving = []
+
     def remote(src, dst, number, target):
         return pltpu.make_async_remote_copy(
             src_ref=src,
@@ -232,18 +238,60 @@
         )
 
     def spread(ref, number):
-        @pl.loop(1, NQ)
+        @pl.loop(0, NQ - 1)
         def _(k):
             mine = ref.at[core, q]
             remote(mine, mine, number, {"row": plane_peer(k)}).start()
 
+        leaving.append((remote, ref.at[core, 0 : NQ - 1], number, {"row": q * 2 + other}))
+
     def spread_wait(ref, number):
         some = ref.at[core, 0 : NQ - 1]
         remote(some, some, number, {"row": q * 2 + other}).wait_recv()
 
+    def along_z(mine, some, number):
+        @pl.loop(0, NZ - 1)
+        def _(k):
+            to = (x * NZ + (z + away(k, NZ)) % NZ) * 2 + core
+            remote(mine, mine, number, {"row": to}).start()
+
+        leaving.append((remote, some, number, {"row": q * 2 + other}))
+
+    def along_x(mine, some, number):
+        @pl.loop(0, NX - 1)
+        def _(k):
+            to = (((x + away(k, NX)) % NX) * NZ + z) * 2 + core
+            remote(mine, mine, number, {"row": to}).start()
+
+        leaving.append((remote, some, number, {"row": q * 2 + other}))
+
+    def landed(some, number):
+        remote(some, some, number, {"row": q * 2 + other}).wait_recv()
+
+    def z_first(ref, number):
+        along_z(ref.at[core, x, z], ref.at[core, 0, 0 : NZ - 1], number)
+
+    def then_x(ref, number):
+        landed(ref.at[core, 0, 0 : NZ - 1], number)
+        along_x(ref.at[core, x], ref.at[core, 0 : NX - 1], number + 1)
+
+    def x_landed(ref, number):
+        landed(ref.at[core, 0 : NX - 1], number + 1)
+
+    def x_first(ref, number):
+        along_x(ref.at[core, x, z], ref.at[core, 0, 0 : NX - 1], number)
+
+    def then_z(ref, number):
+        landed(ref.at[core, 0, 0 : NX - 1], number)
+        along_z(ref.at[core, :, z], ref.at[core, :, 0 : NZ - 1], number + 1)
+
+    def z_landed(ref, number):
+        landed(ref.at[core, :, 0 : NZ - 1], number + 1)
+
     def share(ref, number):
         half = ref.at[core]
         remote(half, half, number, {"row": q * 2 + other}).start()
+        leaving.append((remote, half, number, {"row": q * 2 + other}))
 
     def share_wait(ref, number):
         half = ref.at[other]
@@ -260,10 +308,12 @@
         )
 
     def ring_all(landing, number):
-        @pl.loop(1, NC)
+        @pl.loop(0, NC - 1)
         def _(k):
             mine = landing.at[col]
-            ring(mine, mine, number, (col + k) % NC).start()
+            ring(mine, mine, number, (col + away(k, NC)) % NC).start()
+
+        leaving.append((ring, landing.at[0 : NC - 1], number, (col + 1) % NC))
 
     def ring_wait(landing, number):
         some = landing.at[0 : NC - 1]
@@ -279,11 +329,12 @@
     def reduce_send(number):
         slab, landing = slabs[number], sums[number]
 
-        @pl.loop(1, NC)
+        @pl.loop(0, NC - 1)
         def _(k):
-            to = (col + k) % NC
+            to = (col + away(k, NC)) % NC
             ring(slab.at[to], landing.at[col], number, to).start()
 
+        leaving.append((ring, landing.at[0 : NC - 1], number, (col + 1) % NC))
         landing[col] = slab[col]
 
     def reduced(number, at):
@@ -344,15 +395,10 @@
     def panels(ref, index, b):
         return jnp.concatenate([ref[2 * b, index], ref[2 * b + 1, index]], axis=1)
 
-    def block_of(ref, h, g):
-        if ref.shape[2] == GROUP:
-            return ref[h].reshape(NQ * GROUP, 256)
-        return ref[h, :, g * GROUP : (g + 1) * GROUP].reshape(NQ * GROUP, 256)
-
     def add_forward(t, g, h, ref, entry, start):
         target, at, count = entry
         weights = fw[t][g, h, at : at + count]
-        value = jnp.dot(weights, block_of(ref, h, g), preferred_element_type=F32)
+        value = jnp.dot(weights, ref[h].reshape(NQ * GROUP, 256), preferred_element_type=F32)
         if target < 0:
             base = g * 128
             if start:
@@ -366,7 +412,7 @@
     def add_backward(t, g, h, ref, entry):
         s, at, count = entry
         weights = bw[t][g, h, at : at + count]
-        value = jnp.dot(weights, block_of(ref, h, g), preferred_element_type=F32)
+        value = jnp.dot(weights, ref[h].reshape(NQ * GROUP, 256), preferred_element_type=F32)
         first = g * 128 * 2 ** (s - t)
         acc[s][first : first + count] -= value
 
@@ -380,13 +426,16 @@
     d0 = gather["d0"]
     inside = dw[0] * table(out_row < widths_ref[0])
     panel[col, TD] = inside
-    for i in range(2):
-        d0[i, core, q] = inside[i * GROUP : (i + 1) * GROUP]
+    d0[core, x, z] = inside
     for n in range(1, 3):
         panel[col, TD + n] = dw[n]
-    for t in range(4, 1, -1):
-        for hop in range(t):
-            mask(lw, out_row, t, hop)
+    pl.semaphore_wait(barrier, NQ - 1 + NC - 1 + 1)
+
+    f4, f3, b3 = gather["f4"], gather["f3"], gather["b3"]
+    x_first(f4.at[3], 9)
+    for g in range(3):
+        z_first(f4.at[g], 3 * g)
+    ring_all(panel, PANEL)
 
     e, f = iota((96, GROUP), 0), iota((96, GROUP), 1)
     expanded = table(jnp.logical_and(e // 32 == f // 4, e % 32 == col * 4 + f % 4))
@@ -395,44 +444,28 @@
     pend[1][...] = begun[32:96]
     for t in range(2, 4):
         pend[t][...] = jnp.zeros_like(pend[t])
-    expand_forward(4)
-    pl.semaphore_wait(barrier, NQ - 1 + NC - 1 + 1)
-
-    f4 = gather["f4"]
-    for g in range(4):
-
-        @pl.loop(1, NZ)
-        def _(k):
-            mine = f4.at[g, core, q]
-            remote(mine, mine, 3 * g, {"row": (x * NZ + (z + k) % NZ) * 2 + core}).start()
-
-    ring_all(panel, PANEL)
-    expand_forward(3)
-    expand_forward(2)
-    for g in range(4):
-        some = f4.at[g, core, 0 : NZ - 1]
-        remote(some, some, 3 * g, {"row": q * 2 + other}).wait_recv()
-
-        @pl.loop(1, NX)
-        def _(k):
-            line = f4.at[g, core, pl.ds(x * NZ, NZ)]
-            remote(line, line, 3 * g + 1, {"row": (((x + k) % NX) * NZ + z) * 2 + core}).start()
-
-    for s in range(1, LEVELS):
-        for hop in range(s):
-            if s > 1:
-                mask(uw, in_row, s, hop)
-    @pl.loop(0, 8)
-    def _(b):
-        r, s = iota((128, 256), 0), iota((128, 256), 1)
-        hit = jnp.logical_and(r // 32 == col // 2, s == b * 32 + r % 32)
-        place[pl.ds(pl.multiple_of(b * 128, 128), 128)] = table(hit)
+    mask(lw, out_row, 4, 0)
+    expand_forward(4, FROWS[4][0][:1])
+    then_z(f4.at[3], 9)
+    for t in range(4, 1, -1):
+        for hop in range(t):
+            if (t, hop) != (4, 0):
+                mask(lw, out_row, t, hop)
+    then_x(f4.at[0], 0)
+    expand_forward(4, FROWS[4][0][1:3])
+    then_x(f4.at[1], 3)
+    then_x(f4.at[2], 6)
+    z_first(d0, 12)
+    expand_forward(4, FROWS[4][0][3:])
+    x_landed(f4.at[0], 0)
+    share(f4.at[0], 2)
+    expand_forward(3, FROWS[3][0])
 
     parents = FROWS[4][0][0]
     for g in range(4):
-        some = f4.at[g, core, 0 : NQ - NZ]
-        remote(some, some, 3 * g + 1, {"row": q * 2 + other}).wait_recv()
-        share(f4.at[g], 3 * g + 2)
+        if g > 0:
+            (x_landed if g < 3 else z_landed)(f4.at[g], 3 * g)
+            share(f4.at[g], 3 * g + 2)
         add_forward(4, g, core, f4.at[g], parents, True)
         if g > 0:
             share_wait(f4.at[g - 1], 3 * (g - 1) + 2)
@@ -440,108 +473,131 @@
     share_wait(f4.at[3], 11)
     add_forward(4, 3, other, f4.at[3], parents, False)
     reduce_start(pend[3], 3, R3)
-    spread(d0.at[0], 12)
+    then_x(d0, 12)
     for g in range(4):
         for entry in FROWS[4][0][1:]:
             add_forward(4, g, core, f4.at[g], entry, True)
             add_forward(4, g, other, f4.at[g], entry, False)
 
-    for t, number, ringed in ((3, 14, R3), (2, 16, R2)):
-        ref = gather[f"f{t}"]
-        ring_wait(sums[ringed], ringed)
-        for g in range(GROUPS[t]):
-            at = slice(g * GROUP, (g + 1) * GROUP)
-            y = rows_in[piece(t, g)].astype(F32) - reduced(ringed, at)
-            ref[core, q, at] = (valid(t, g) * y).astype(BF)
-        spread(ref, number)
-        if t == 3:
-            ring_wait(panel, PANEL)
-            for g in range(2):
-                for n in range(2):
-                    left = jnp.concatenate([panel[4 * g + j, TU + n] for j in range(4)], axis=1)
-
-                    @pl.loop(0, 2)
-                    def _(h):
-                        wide_u[g, h, n * 32 : n * 32 + 32] = expand(left, h, 0, 4).astype(BF)
-
-            left = jnp.concatenate(
-                [
-                    jnp.concatenate([panels(panel, TL, b), panels(panel, TL + 1, b)], axis=1)
-                    for b in range(4)
-                ],
-                axis=0,
-            )
-
-            @pl.loop(0, 2)
-            def _(h):
-                top1[h, 0:128] = expand(left, h, 0, 4).astype(BF)
-
-            for n in range(3):
-                left = jnp.concatenate([panels(panel, TD + n, b) for b in range(4)], axis=0)
-
-                @pl.loop(0, 2)
-                def _(h):
-                    if n == 0:
-                        top0[h, 0:128] = expand(left, h, 0, 2).astype(BF)
-                    else:
-                        wide = expand(left, h, 2 * n - 2, 2 * n).astype(BF)
-                        top1[h, n * 128 : n * 128 + 128] = wide
-
-        else:
-            expand_backward(1)
-        spread_wait(ref, number)
-        share(ref, number + 1)
-        parents = FROWS[t][0][0]
-        for g in range(GROUPS[t]):
-            add_forward(t, g, core, ref, parents, True)
-        share_wait(ref, number + 1)
-        for g in range(GROUPS[t]):
-            add_forward(t, g, other, ref, parents, False)
-        if t == 3:
-            reduce_start(pend[2], 2, R2)
-            spread_wait(d0.at[0], 12)
-            share(d0.at[0], 13)
-            spread(d0.at[1], 18)
-        else:
-            split_start(1, P1)
-        for g in range(GROUPS[t]):
-            for entry in FROWS[t][0][1:]:
-                add_forward(t, g, core, ref, entry, True)
-                add_forward(t, g, other, ref, entry, False)
+    ring_wait(sums[R3], R3)
+    for g in range(2):
+        y = rows_in[piece(3, g)].astype(F32) - reduced(R3, slice(g * GROUP, (g + 1) * GROUP))
+        f3[g, core, x, z] = (valid(3, g) * y).astype(BF)
+    x_first(f3.at[1], 17)
+    z_first(f3.at[0], 14)
+    expand_forward(2, FROWS[2][0])
+    then_z(f3.at[1], 17)
+    ring_wait(panel, PANEL)
+    left = jnp.concatenate(
+        [
+            jnp.concatenate([panels(panel, TL, b), panels(panel, TL + 1, b)], axis=1)
+            for b in range(4)
+        ],
+        axis=0,
+    )
+
+    @pl.loop(0, 2)
+    def _(h):
+        top1[h, 0:128] = expand(left, h, 0, 4).astype(BF)
+
+    then_x(f3.at[0], 14)
+    x_landed(d0, 12)
+    share(d0, 32)
+    for g in range(2):
+        left = jnp.concatenate(
+            [
+                jnp.concatenate([panel[4 * g + j, TU + n] for j in range(4)], axis=1)
+                for n in range(2)
+            ],
+            axis=0,
+        )
+
+        @pl.loop(0, 2)
+        def _(h):
+            wide_u[g, h] = expand(left, h, 0, 4).astype(BF)
+
+    for n in range(3):
+        left = jnp.concatenate([panels(panel, TD + n, b) for b in range(4)], axis=0)
+
+        @pl.loop(0, 2)
+        def _(h):
+            if n == 0:
+                top0[h, 0:128] = expand(left, h, 0, 2).astype(BF)
+            else:
+                wide = expand(left, h, 2 * n - 2, 2 * n).astype(BF)
+                top1[h, n * 128 : n * 128 + 128] = wide
+
+    parents = FROWS[3][0][0]
+    x_landed(f3.at[0], 14)
+    share(f3.at[0], 16)
+    add_forward(3, 0, core, f3.at[0], parents, True)
+    z_landed(f3.at[1], 17)
+    share(f3.at[1], 19)
+    share_wait(f3.at[0], 16)
+    add_forward(3, 0, other, f3.at[0], parents, False)
+    add_forward(3, 1, core, f3.at[1], parents, True)
+    share_wait(f3.at[1], 19)
+    add_forward(3, 1, other, f3.at[1], parents, False)
+    reduce_start(pend[2], 2, R2)
+    for g in range(2):
+        for entry in FROWS[3][0][1:]:
+            add_forward(3, g, core, f3.at[g], entry, True)
+            add_forward(3, g, other, f3.at[g], entry, False)
+    share_wait(d0, 32)
+    product = jnp.zeros((64, 256), F32)
+    for g in range(2):
+        for h in range(2):
+            block = d0[h, :, :, g * GROUP : (g + 1) * GROUP].reshape(NQ * GROUP, 256)
+            product = product + jnp.dot(wide_u[g, h], block, preferred_element_type=F32)
+    mpanel[col] = product.astype(BF).reshape(2, 32, 256)
+
+    ref = gather["f2"]
+    ring_wait(sums[R2], R2)
+    y = rows_in[piece(2, 0)].astype(F32) - reduced(R2, slice(0, GROUP))
+    ref[core, q] = (valid(2, 0) * y).astype(BF)
+    spread(ref, 20)
+    ring_all(mpanel, MPANEL)
+    for s in range(2, LEVELS):
+        for hop in range(s):
+            mask(uw, in_row, s, hop)
+    expand_backward(1)
+    spread_wait(ref, 20)
+    share(ref, 21)
+    parents = FROWS[2][0][0]
+    add_forward(2, 0, core, ref, parents, True)
+    share_wait(ref, 21)
+    add_forward(2, 0, other, ref, parents, False)
+    split_start(1, P1)
+    for entry in FROWS[2][0][1:]:
+        add_forward(2, 0, core, ref, entry, True)
+        add_forward(2, 0, other, ref, entry, False)
 
     split_start(0, P0)
-    spread_wait(d0.at[1], 18)
-    share(d0.at[1], 19)
+    @pl.loop(0, 8)
+    def _(b):
+        r, s = iota((128, 256), 0), iota((128, 256), 1)
+        hit = jnp.logical_and(r // 32 == col // 2, s == b * 32 + r % 32)
+        place[pl.ds(pl.multiple_of(b * 128, 128), 128)] = table(hit)
+
     y1 = gather["y1"]
     ring_wait(sums[P1], P1)
     solved = -reduced(P1, slice(0, GROUP))
     for n in range(2):
-        solved_n = valid_top(1 + n) * solved[n * 8 : n * 8 + 8]
-        packed[n * 8 : n * 8 + 8] = solved_n
+        packed[n * 8 : n * 8 + 8] = valid_top(1 + n) * solved[n * 8 : n * 8 + 8]
     y1[core, q] = packed[...].astype(BF)
-    spread(y1, 20)
-    share_wait(d0.at[0], 13)
-    share_wait(d0.at[1], 19)
-    product = jnp.zeros((64, 256), F32)
-    for g in range(2):
-        for h in range(2):
-            product = product + jnp.dot(
-                wide_u[g, h], d0[g, h].reshape(NQ * GROUP, 256), preferred_element_type=F32
-            )
-    mpanel[col] = product.astype(BF).reshape(2, 32, 256)
-    ring_all(mpanel, MPANEL)
+    spread(y1, 22)
     expand_backward(2)
     ring_wait(sums[P0], P0)
-    spread_wait(y1, 20)
-    share(y1, 21)
-    share_wait(y1, 21)
+    spread_wait(y1, 22)
+    share(y1, 23)
+    share_wait(y1, 23)
     y0 = -reduced(P0, slice(0, 8)) - fold(top_product(top1, y1, 0, 128))
     y0 = valid_top(0) * y0
     ref = gather["y0"]
     packed[0:8] = y0
     packed[8:16] = jnp.zeros((8, 128), F32)
     ref[core, q] = packed[...].astype(BF)
-    spread(ref, 22)
+    spread(ref, 24)
     wide = top_product(top1, y1, 128, 256)
     scaled = [fold(wide[n * 128 : n * 128 + 128]) for n in range(2)]
     ring_wait(mpanel, MPANEL)
@@ -554,9 +610,9 @@
             top0[h, 128 + n * 128 : 256 + n * 128] = wide
 
     expand_backward(3)
-    spread_wait(ref, 22)
-    share(ref, 23)
-    share_wait(ref, 23)
+    spread_wait(ref, 24)
+    share(ref, 25)
+    share_wait(ref, 25)
     wide = top_product(top0, ref, 0, 384)
     split[col, 0:8] = (valid_top(0) * fold(wide[0:128])).astype(BF)
     for n in range(2):
@@ -574,75 +630,70 @@
     rows_out[piece(0, 0)] = solved
 
     gather["b1"][core, q] = solved
-    for t, number, ringed in ((1, 24, None), (2, 26, B2), (3, 28, B3), (4, None, B4)):
-        if t > 1:
-            ring_wait(sums[ringed], ringed)
-            for g in range(GROUPS[t]):
-                at = slice(g * GROUP, (g + 1) * GROUP)
-                solved = (valid(t, g) * reduced(ringed, at)).astype(BF)
-                rows_out[piece(t, g)] = solved
-                if t < 4:
-                    gather[f"b{t}"][core, q, at] = solved
-        if t == 4:
-            break
+    for t, number, ringed in ((1, 26, None), (2, 28, B2)):
         ref = gather[f"b{t}"]
+        if t == 2:
+            ring_wait(sums[B2], B2)
+            solved = (valid(2, 0) * reduced(B2, slice(0, GROUP))).astype(BF)
+            rows_out[piece(2, 0)] = solved
+            ref[core, q] = solved
         spread(ref, number)
         spread_wait(ref, number)
         share(ref, number + 1)
         children = BROWS[t][0][0]
-        for g in range(GROUPS[t]):
-            add_backward(t, g, core, ref, children)
+        add_backward(t, 0, core, ref, children)
         share_wait(ref, number + 1)
-        for g in range(GROUPS[t]):
-            add_backward(t, g, other, ref, children)
-        reduce_start(acc[t + 1], t + 1, {1: B2, 2: B3, 3: B4}[t])
-        for g in range(GROUPS[t]):
-            for entry in BROWS[t][0][1:]:
-                add_backward(t, g, core, ref, entry)
-                add_backward(t, g, other, ref, entry)
+        add_backward(t, 0, other, ref, children)
+        reduce_start(acc[t + 1], t + 1, {1: B2, 2: B3}[t])
+        for entry in BROWS[t][0][1:]:
+            add_backward(t, 0, core, ref, entry)
+            add_backward(t, 0, other, ref, entry)
+    ring_wait(sums[B3], B3)
+    for g in range(2):
+        solved = (valid(3, g) * reduced(B3, slice(g * GROUP, (g + 1) * GROUP))).astype(BF)
+        rows_out[piece(3, g)] = solved
+        b3[g, core, x, z] = solved
+    x_first(b3.at[1], 33)
+    z_first(b3.at[0], 30)
+    then_z(b3.at[1], 33)
+    then_x(b3.at[0], 30)
+    children = BROWS[3][0][0]
+    x_landed(b3.at[0], 30)
+    share(b3.at[0], 35)
+    add_backward(3, 0, core, b3.at[0], children)
+    z_landed(b3.at[1], 33)
+    share(b3.at[1], 36)
+    share_wait(b3.at[0], 35)
+    add_backward(3, 0, other, b3.at[0], children)
+    add_backward(3, 1, core, b3.at[1], children)
+    share_wait(b3.at[1], 36)
+    add_backward(3, 1, other, b3.at[1], children)
+    reduce_start(acc[4], 4, B4)
+    ring_wait(sums[B4], B4)
+    for g in range(4):
+        solved = valid(4, g) * reduced(B4, slice(g * GROUP, (g + 1) * GROUP))
+        rows_out[piece(4, g)] = solved.astype(BF)
 
     order = table(iota((128, 128), 0) == heap_row(iota((128, 128), 1)))
-    answer = jnp.dot(order, rows_out[...], preferred_element_type=F32).astype(BF)
-    out_ref[...] = answer[0:124]
-
-    for g in range(4):
-        sent = f4.at[g, core, 0 : NZ - 1]
-        remote(sent, sent, 3 * g, {"row": q * 2 + other}).wait_send()
-        sent = f4.at[g, core, 0 : NQ - NZ]
-        remote(sent, sent, 3 * g + 1, {"row": q * 2 + other}).wait_send()
-        sent = f4.at[g, core]
-        remote(sent, sent, 3 * g + 2, {"row": q * 2 + other}).wait_send()
-    for ref, first, second in (
-        (d0.at[0], 12, 13),
-        (gather["f3"], 14, 15),
-        (gather["f2"], 16, 17),
-        (d0.at[1], 18, 19),
-        (gather["y1"], 20, 21),
-        (gather["y0"], 22, 23),
-        (gather["b1"], 24, 25),
-        (gather["b2"], 26, 27),
-        (gather["b3"], 28, 29),
-    ):
-        sent = ref.at[core, 0 : NQ - 1]
-        remote(sent, sent, first, {"row": q * 2 + other}).wait_send()
-        sent = ref.at[core]
-        remote(sent, sent, second, {"row": q * 2 + other}).wait_send()
-    for number in range(RINGS):
-        landing = {SPLIT: split, PANEL: panel, MPANEL: mpanel}.get(number)
-        landing = sums[number] if landing is None else landing
-        sent = landing.at[0 : NC - 1]
-        ring(sent, sent, number, (col + 1) % NC).wait_send()
+    heap[...] = jnp.dot(order, rows_out[...], preferred_element_type=F32)
+    for n in range(31):
+        out_ref[n] = heap[4 * n : 4 * n + 4].astype(BF)
+
+    for kind, ref, number, target in leaving:
+        kind(ref, ref, number, target).wait_send()
 
 
 def scratch_shapes():
     gather = {
-        "f4": pltpu.VMEM((4, 2, NQ, GROUP, 256), BF),
-        "d0": pltpu.VMEM((2, 2, NQ, GROUP, 256), BF),
+        "f4": pltpu.VMEM((4, 2, NX, NZ, GROUP, 256), BF),
+        "f3": pltpu.VMEM((2, 2, NX, NZ, GROUP, 256), BF),
+        "b3": pltpu.VMEM((2, 2, NX, NZ, GROUP, 256), BF),
+        "d0": pltpu.VMEM((2, NX, NZ, 2 * GROUP, 256), BF),
         "y1": pltpu.VMEM((2, NQ, GROUP, 128), BF),
         "y0": pltpu.VMEM((2, NQ, GROUP, 128), BF),
     }
-    for name, t in (("f3", 3), ("f2", 2), ("b1", 1), ("b2", 2), ("b3", 3)):
-        gather[name] = pltpu.VMEM((2, NQ, GROUP * GROUPS[t], 256), BF)
+    for name in ("f2", "b1", "b2"):
+        gather[name] = pltpu.VMEM((2, NQ, GROUP, 256), BF)
     slabs = {n: pltpu.VMEM((NC, GROUP * k, 256), BF) for n, k in ((R3, 2), (R2, 1), (B2, 1), (B3, 2), (B4, 4))}
     slabs[P1] = pltpu.VMEM((NC, GROUP, 128), BF)
     slabs[P0] = pltpu.VMEM((NC, 8, 128), F32)
@@ -652,6 +703,7 @@
         "dw": pltpu.VMEM((31, 32, 256), BF),
         "rows_in": pltpu.VMEM((128, 256), BF),
         "rows_out": pltpu.VMEM((128, 256), BF),
+        "heap": pltpu.VMEM((128, 256), F32),
         "sel": pltpu.VMEM((2, 1024, 512), BF),
         "perm": pltpu.VMEM((128, 128), BF),
         "place": pltpu.VMEM((1024, 256), BF),
@@ -669,14 +721,13 @@
         "gather": gather,
         "slabs": slabs,
         "sums": dict(slabs),
-        "relay_sem": pltpu.SemaphoreType.DMA((2, 30)),
+        "relay_sem": pltpu.SemaphoreType.DMA((2, 37)),
         "ring_sem": pltpu.SemaphoreType.DMA((2, RINGS)),
         "load_sem": pltpu.SemaphoreType.DMA((3,)),
     }
 
 
 def shards(right_side, lower_blocks, upper_blocks, pivot_inverse, widths, first_row):
-    nodes, rows, columns = right_side.shape
     vmem = pl.BlockSpec(memory_space=pltpu.VMEM)
     smem = pl.BlockSpec(memory_space=pltpu.SMEM)
     hbm = pl.BlockSpec(memory_space=pl.ANY)
@@ -685,9 +736,9 @@
     def body(*refs):
         kernel(*refs[:7], jax.tree.unflatten(tree, refs[7:]))
 
-    answer = pl.pallas_call(
+    return pl.pallas_call(
         body,
-        out_shape=jax.ShapeDtypeStruct((nodes * rows, columns), BF),
+        out_shape=jax.ShapeDtypeStruct(right_side.shape, BF),
         in_specs=[vmem, smem, smem, hbm, hbm, hbm],
         out_specs=vmem,
         scratch_shapes=leaves,
@@ -696,14 +747,13 @@
         ),
         name="tree_solve",
     )(
-        right_side.reshape(nodes * rows, columns),
+        right_side,
         widths,
-        first_row,
+        first_row.T,
         lower_blocks,
         upper_blocks,
         pivot_inverse,
     )
-    return answer.reshape(nodes, rows, columns)
 
 
 def solution(mesh):

time: 180 us -> 152 us (0.84)
  Pallas kernels: 176 us -> 150 us
  local copies, waits for them, and re-layouts: 4.33 us -> 1.48 us
    pallas_call x1, Pallas kernels: 176 us -> 150 us  [shards(): pl.pallas_call(body, out_shape=jax.ShapeDtypeStruct(right_side.shape, BF)...]
    reshape x2 -> x0, local copies, waits for them, and re-layouts: 2.96 us -> none  [the longest x1 1.48 us: shards(): return answer.reshape(nodes, rows, columns)]
where the time goes in v3:
time: 152 us
  Pallas kernels  150 us (99%)
    pallas_call x1, Pallas kernels, shards(): pl.pallas_call(body, out_shape=jax.ShapeDtypeStruct(right_side.shape, BF)...  150 us

profile of v3, /device:TPU:1, one launch (start us, length us, event | category | flops | bytes accessed | tf_op | source)
XLA Modules:
  0.0 151.6 jit_solution(13620670323298469362)
XLA Ops:
  0.0 150.1 %tree_solve.1 = bf16[31,4,256]{2,1,0:T(4,128)(2,1)} custom-call(bf16[31,4,256]{2,1,0:T(4,128)(2,1)} %refs_0_.1, s32[31]{0:T(128)} %refs_1_.1, s32[4,31]{1,0:T(4,128)} %bitcast.1, bf16[98,32,256]{2,1,0:T(8,128)(2,1)} %refs_3_.1, bf16[98,32,256]{2,1,0:T(8,128)(2,1)} %refs_4_.1, bf16[31,32,256]{2,1,0:T(8,128)(2,1)} %refs_5_.1), custom_call_target="tpu_custom_call" | custom-call | tf_op jit(solution)/shard_map/tree_solve/pallas_call | solution.py:739
  150.1 1.5 copy.8

commit v4 on v3

--- a/solution.py
+++ b/solution.py
@@ -55,7 +55,7 @@
 FROWS = {t: forward_rows(t) for t in range(TOP, LEVELS)}
 BROWS = {t: backward_rows(t) for t in range(1, LEVELS - 1)}
 TL, TU, TD, TOPS = 0, 2, 4, 7
-R3, R2, P1, P0, SPLIT, B2, B3, B4, PANEL, MPANEL, RINGS = range(11)
+R3, R3B, R2, P1, P0, SPLIT, B2, B3, B3B, B4, B4B, PANEL, MPANEL, RINGS = range(14)
 
 
 def kernel(rs_ref, widths_ref, first_ref, l_hbm, u_hbm, d_hbm, out_ref, scratch):
@@ -86,7 +86,7 @@
         return (n // 2 + (k + 1) // 2 * (1 - 2 * ((k + 1) % 2))) % n
 
     def plane_peer(k):
-        px, pz = (x + away(k % NX, NX)) % NX, (z + away(k // NX, NZ)) % NZ
+        px, pz = (x + away(k // NZ, NX)) % NX, (z + away(k % NZ, NZ)) % NZ
         return (px * NZ + pz) * 2 + core
 
     def signal(target):
@@ -319,9 +319,9 @@
         some = landing.at[0 : NC - 1]
         ring(some, some, number, (col + 1) % NC).wait_recv()
 
-    def reduce_start(source, t, number):
-        for g in range(GROUPS[t]):
-            part = source[g * 128 : (g + 1) * 128].astype(BF)
+    def reduce_start(source, first, groups, number):
+        for g in range(groups):
+            part = source[(first + g) * 128 : (first + g + 1) * 128].astype(BF)
             cut = jnp.dot(perm[...], part, preferred_element_type=F32).astype(BF)
             slabs[number][:, g * GROUP : (g + 1) * GROUP] = cut.reshape(NC, GROUP, 256)
         reduce_send(number)
@@ -457,35 +457,34 @@
     then_x(f4.at[2], 6)
     z_first(d0, 12)
     expand_forward(4, FROWS[4][0][3:])
-    x_landed(f4.at[0], 0)
-    share(f4.at[0], 2)
-    expand_forward(3, FROWS[3][0])
-
     parents = FROWS[4][0][0]
     for g in range(4):
+        (x_landed if g < 3 else z_landed)(f4.at[g], 3 * g)
+        share(f4.at[g], 3 * g + 2)
         if g > 0:
-            (x_landed if g < 3 else z_landed)(f4.at[g], 3 * g)
-            share(f4.at[g], 3 * g + 2)
-        add_forward(4, g, core, f4.at[g], parents, True)
-        if g > 0:
-            share_wait(f4.at[g - 1], 3 * (g - 1) + 2)
-            add_forward(4, g - 1, other, f4.at[g - 1], parents, False)
-    share_wait(f4.at[3], 11)
-    add_forward(4, 3, other, f4.at[3], parents, False)
-    reduce_start(pend[3], 3, R3)
+            add_forward(4, g - 1, core, f4.at[g - 1], parents, True)
+    for g in range(4):
+        share_wait(f4.at[g], 3 * g + 2)
+        add_forward(4, g, other, f4.at[g], parents, False)
+        if g == 1:
+            reduce_start(pend[3], 0, 1, R3)
+            add_forward(4, 3, core, f4.at[3], parents, True)
+    reduce_start(pend[3], 1, 1, R3B)
     then_x(d0, 12)
     for g in range(4):
         for entry in FROWS[4][0][1:]:
             add_forward(4, g, core, f4.at[g], entry, True)
             add_forward(4, g, other, f4.at[g], entry, False)
 
-    ring_wait(sums[R3], R3)
-    for g in range(2):
-        y = rows_in[piece(3, g)].astype(F32) - reduced(R3, slice(g * GROUP, (g + 1) * GROUP))
+    expand_forward(3, FROWS[3][0])
+
+    for g, number in enumerate((R3, R3B)):
+        ring_wait(sums[number], number)
+        y = rows_in[piece(3, g)].astype(F32) - reduced(number, slice(0, GROUP))
         f3[g, core, x, z] = (valid(3, g) * y).astype(BF)
+        if g == 0:
+            z_first(f3.at[0], 14)
     x_first(f3.at[1], 17)
-    z_first(f3.at[0], 14)
-    expand_forward(2, FROWS[2][0])
     then_z(f3.at[1], 17)
     ring_wait(panel, PANEL)
     left = jnp.concatenate(
@@ -538,11 +537,12 @@
     add_forward(3, 1, core, f3.at[1], parents, True)
     share_wait(f3.at[1], 19)
     add_forward(3, 1, other, f3.at[1], parents, False)
-    reduce_start(pend[2], 2, R2)
+    reduce_start(pend[2], 0, 1, R2)
     for g in range(2):
         for entry in FROWS[3][0][1:]:
             add_forward(3, g, core, f3.at[g], entry, True)
             add_forward(3, g, other, f3.at[g], entry, False)
+    expand_forward(2, FROWS[2][0])
     share_wait(d0, 32)
     product = jnp.zeros((64, 256), F32)
     for g in range(2):
@@ -644,17 +644,20 @@
         add_backward(t, 0, core, ref, children)
         share_wait(ref, number + 1)
         add_backward(t, 0, other, ref, children)
-        reduce_start(acc[t + 1], t + 1, {1: B2, 2: B3}[t])
+        reduce_start(acc[t + 1], 0, 1, {1: B2, 2: B3}[t])
+        if t == 2:
+            reduce_start(acc[3], 1, 1, B3B)
         for entry in BROWS[t][0][1:]:
             add_backward(t, 0, core, ref, entry)
             add_backward(t, 0, other, ref, entry)
-    ring_wait(sums[B3], B3)
-    for g in range(2):
-        solved = (valid(3, g) * reduced(B3, slice(g * GROUP, (g + 1) * GROUP))).astype(BF)
+    for g, number in enumerate((B3, B3B)):
+        ring_wait(sums[number], number)
+        solved = (valid(3, g) * reduced(number, slice(0, GROUP))).astype(BF)
         rows_out[piece(3, g)] = solved
         b3[g, core, x, z] = solved
+        if g == 0:
+            z_first(b3.at[0], 30)
     x_first(b3.at[1], 33)
-    z_first(b3.at[0], 30)
     then_z(b3.at[1], 33)
     then_x(b3.at[0], 30)
     children = BROWS[3][0][0]
@@ -665,14 +668,17 @@
     share(b3.at[1], 36)
     share_wait(b3.at[0], 35)
     add_backward(3, 0, other, b3.at[0], children)
+    reduce_start(acc[4], 0, 2, B4)
     add_backward(3, 1, core, b3.at[1], children)
     share_wait(b3.at[1], 36)
     add_backward(3, 1, other, b3.at[1], children)
-    reduce_start(acc[4], 4, B4)
-    ring_wait(sums[B4], B4)
+    reduce_start(acc[4], 2, 2, B4B)
     for g in range(4):
-        solved = valid(4, g) * reduced(B4, slice(g * GROUP, (g + 1) * GROUP))
-        rows_out[piece(4, g)] = solved.astype(BF)
+        number = (B4, B4B)[g // 2]
+        if g % 2 == 0:
+            ring_wait(sums[number], number)
+        at = slice(g % 2 * GROUP, (g % 2 + 1) * GROUP)
+        rows_out[piece(4, g)] = (valid(4, g) * reduced(number, at)).astype(BF)
 
     order = table(iota((128, 128), 0) == heap_row(iota((128, 128), 1)))
     heap[...] = jnp.dot(order, rows_out[...], preferred_element_type=F32)
@@ -694,7 +700,8 @@
     }
     for name in ("f2", "b1", "b2"):
         gather[name] = pltpu.VMEM((2, NQ, GROUP, 256), BF)
-    slabs = {n: pltpu.VMEM((NC, GROUP * k, 256), BF) for n, k in ((R3, 2), (R2, 1), (B2, 1), (B3, 2), (B4, 4))}
+    slabs = {n: pltpu.VMEM((NC, GROUP, 256), BF) for n in (R3, R3B, R2, B2, B3, B3B)}
+    slabs |= {n: pltpu.VMEM((NC, 2 * GROUP, 256), BF) for n in (B4, B4B)}
     slabs[P1] = pltpu.VMEM((NC, GROUP, 128), BF)
     slabs[P0] = pltpu.VMEM((NC, 8, 128), F32)
     return {

time: 152 us -> 148 us (0.974)
  Pallas kernels: 150 us -> 147 us
    pallas_call x1, Pallas kernels: 150 us -> 147 us  [shards(): pl.pallas_call(body, out_shape=jax.ShapeDtypeStruct(right_side.shape, BF)...]
where the time goes in v4:
time: 148 us
  Pallas kernels  147 us (99%)
  local copies, waits for them, and re-layouts  1.48 us (1%)
    pallas_call x1, Pallas kernels, shards(): pl.pallas_call(body, out_shape=jax.ShapeDtypeStruct(right_side.shape, BF)...  147 us

profile of v4, /device:TPU:1, one launch (start us, length us, event | category | flops | bytes accessed | tf_op | source)
XLA Modules:
  0.0 148.2 jit_solution(13063982886634453790)
XLA Ops:
  0.0 146.7 %tree_solve.1 = bf16[31,4,256]{2,1,0:T(4,128)(2,1)} custom-call(bf16[31,4,256]{2,1,0:T(4,128)(2,1)} %refs_0_.1, s32[31]{0:T(128)} %refs_1_.1, s32[4,31]{1,0:T(4,128)} %bitcast.1, bf16[98,32,256]{2,1,0:T(8,128)(2,1)} %refs_3_.1, bf16[98,32,256]{2,1,0:T(8,128)(2,1)} %refs_4_.1, bf16[31,32,256]{2,1,0:T(8,128)(2,1)} %refs_5_.1), custom_call_target="tpu_custom_call" | custom-call | tf_op jit(solution)/shard_map/tree_solve/pallas_call | solution.py:746
  146.7 1.5 %copy.8 = bf16[31,4,256]{2,1,0:T(4,128)(2,1)} copy(bf16[31,4,256]{2,1,0:T(4,128)(2,1)} %tree_solve.1) | data formatting | bytes 126976
